TPU v7x, 32 devices: a whole 2x2x4 slice. The times are simulated.
32 devices in a mesh: rep: 2 (over x), tm: 16 (over z, y, core).
Axes of the slice: x: 2, y: 2, z: 4, core: 2. Of those that a mesh axis runs over, the one named last changes fastest.
Arguments:
- exo_tokens: bfloat16 [2048, 32, 1024], P('rep', 'tm'), parts along dimension 0, may hold values from -6 to 6
- queries: bfloat16 [2048, 1024], P(('rep', 'tm')), parts along dimension 0, may hold values from -80 to 80, as said below
- key_weight: bfloat16 [1024, 1024], replicated, may hold values from -0.1875 to 0.1875
- value_weight: bfloat16 [1024, 1024], replicated, may hold values from -0.1875 to 0.1875
- out_weight: bfloat16 [1024, 1024], replicated, may hold values from -0.1875 to 0.1875
- gaze_valid: int32 [2048], P(('rep', 'tm')), parts along dimension 0, may hold values 0 or 1
- window_offset: int32 [2048], P(('rep', 'tm')), parts along dimension 0, may hold values from 0 to 16
- cotangent: bfloat16 [2048, 1024], P(('rep', 'tm')), parts along dimension 0, may hold values from -6 to 6
Outputs:
- attended: bfloat16 [2048, 1024], P(('rep', 'tm')), parts along dimension 0
- d_queries: bfloat16 [2048, 1024], P(('rep', 'tm')), parts along dimension 0
- d_key_weight: float32 [2048, 1024], P(('rep', 'tm')), parts along dimension 0
- d_value_weight: float32 [2048, 1024], P(('rep', 'tm')), parts along dimension 0
- d_out_weight: float32 [2048, 1024], P(('rep', 'tm')), parts along dimension 0
There are 2 independent parts, one for each index of `rep`. A program takes and returns all parts, laid end to end along the dimension named above; an argument that names none is the same for every part. Nothing has to cross between parts.
Inputs may be any that keep to these rules, and one draw needn't show every extreme that they name: `queries`: ego gaze query vectors.
All inputs are finite; a program needn't handle non-finite values. No bound on the sum of `gaze_valid` on one device may be relied on, other than what follows from the above.
Results may differ from a plain program's by a relative error of at most 0.025.
The roundings to bfloat16 on the way count: a program that leaves them out, or rounds other values in their place, can miss the bound.
Values may be sent and summed in bfloat16 or wider, within the bound.
A program may use at most 192 MiB of HBM per device.

v0:
```python
import jax
import jax.numpy as jnp
from jax import lax
from jax.sharding import PartitionSpec as P

H = 16
HD = 64
W = 16


def with_halo(block, sides, width):
    for axis, dim in sides:
        count = lax.axis_size(axis)
        forward = [(i, i + 1) for i in range(count - 1)]
        backward = [(target, source) for source, target in forward]
        low = lax.ppermute(
            lax.slice_in_dim(block, block.shape[dim] - width, None, axis=dim), axis, forward
        )
        high = lax.ppermute(lax.slice_in_dim(block, 0, width, axis=dim), axis, backward)
        block = jnp.concatenate([low, block, high], axis=dim)
    return block


def attend_block(
    q_rows, keys, values, grad_rows, valid_rows, offset_rows, out_weight, first, total
):
    n_query = q_rows.shape[0]
    n_frames = keys.shape[0]
    n_tok = keys.shape[1]
    width = q_rows.shape[1]
    scale = HD ** (-0.5)
    t_abs = first + jnp.arange(n_query, dtype=jnp.int32)
    f_abs = first - W + jnp.arange(n_frames, dtype=jnp.int32)
    lower = t_abs - W + offset_rows
    upper = t_abs + offset_rows
    allow = (f_abs[None, :] >= lower[:, None]) & (f_abs[None, :] <= upper[:, None])
    allow = allow & (f_abs[None, :] >= 0) & (f_abs[None, :] < total)
    allow_keys = jnp.repeat(allow, n_tok, axis=1)
    q_heads = q_rows.reshape(n_query, H, HD)
    k_heads = keys.reshape(n_frames * n_tok, H, HD)
    v_heads = values.reshape(n_frames * n_tok, H, HD)
    scores = (
        jnp.einsum("thd,khd->htk", q_heads, k_heads, preferred_element_type=jnp.float32) * scale
    )
    scores = jnp.where(allow_keys[None], scores, -1e30)
    top = jnp.max(scores, axis=-1, keepdims=True)
    expo = jnp.exp(scores - top)
    probs = expo / jnp.sum(expo, axis=-1, keepdims=True)
    probs_b = probs.astype(jnp.bfloat16)
    context = jnp.einsum("htk,khd->thd", probs_b, v_heads, preferred_element_type=jnp.float32)
    context = context.reshape(n_query, width).astype(jnp.bfloat16)
    valid_col = valid_rows.astype(jnp.float32)[:, None]
    attended = (
        jnp.dot(context, out_weight, preferred_element_type=jnp.float32) * valid_col
    ).astype(jnp.bfloat16)
    masked_grad = (grad_rows.astype(jnp.float32) * valid_col).astype(jnp.bfloat16)
    d_context = lax.dot_general(
        masked_grad, out_weight, (((1,), (1,)), ((), ())), preferred_element_type=jnp.float32
    )
    d_context = d_context.astype(jnp.bfloat16)
    d_heads = d_context.reshape(n_query, H, HD)
    d_probs = jnp.einsum("thd,khd->htk", d_heads, v_heads, preferred_element_type=jnp.float32)
    d_scores = probs * (d_probs - jnp.sum(probs * d_probs, axis=-1, keepdims=True)) * scale
    d_scores = d_scores.astype(jnp.bfloat16)
    d_query = jnp.einsum("htk,khd->thd", d_scores, k_heads, preferred_element_type=jnp.float32)
    d_query = d_query.reshape(n_query, width).astype(jnp.bfloat16)
    key_part = jnp.einsum("htk,thd->khd", d_scores, q_heads, preferred_element_type=jnp.float32)
    key_part = key_part.reshape(n_frames, n_tok, width).astype(jnp.bfloat16)
    value_part = jnp.einsum("htk,thd->khd", probs_b, d_heads, preferred_element_type=jnp.float32)
    value_part = value_part.reshape(n_frames, n_tok, width).astype(jnp.bfloat16)
    return (attended, d_query, key_part, value_part, context, masked_grad)


def shards(
    exo_tokens, queries, key_weight, value_weight, out_weight, gaze_valid, window_offset, cotangent
):
    rows_here = queries.shape[0]
    width = queries.shape[1]
    total = rows_here * lax.axis_size("tm")
    first = lax.axis_index("tm") * rows_here
    frame_block = lax.all_to_all(exo_tokens, "tm", split_axis=0, concat_axis=1, tiled=True)
    n_tok = frame_block.shape[1]
    tokens_wide = with_halo(frame_block, (("tm", 0),), W)
    flat = tokens_wide.reshape(-1, width)
    key_rows = jnp.dot(flat, key_weight, preferred_element_type=jnp.float32).astype(jnp.bfloat16)
    value_rows = jnp.dot(flat, value_weight, preferred_element_type=jnp.float32).astype(
        jnp.bfloat16
    )
    paired = jnp.stack([key_rows, value_rows], axis=1).reshape(
        tokens_wide.shape[0], n_tok, 2, width
    )
    attended, d_query, key_part, value_part, context, masked_grad = attend_block(
        queries,
        paired[:, :, 0],
        paired[:, :, 1],
        cotangent,
        gaze_valid,
        window_offset,
        out_weight,
        first,
        total,
    )
    grad_pairs = jnp.stack([key_part, value_part], axis=2)
    flat_sources = tokens_wide.reshape(-1, width)
    flat_grads = grad_pairs.reshape(-1, 2 * width)
    weight_share = lax.psum_scatter(
        lax.dot_general(
            flat_sources, flat_grads, (((0,), (0,)), ((), ())), preferred_element_type=jnp.float32
        ).astype(jnp.bfloat16),
        "tm",
        scatter_dimension=0,
        tiled=True,
    ).astype(jnp.float32)
    out_term = lax.dot_general(
        context, masked_grad, (((0,), (0,)), ((), ())), preferred_element_type=jnp.float32
    )
    d_out_weight = lax.psum_scatter(
        out_term.astype(jnp.bfloat16), "tm", scatter_dimension=0, tiled=True
    ).astype(jnp.float32)
    return (attended, d_query, weight_share[:, :width], weight_share[:, width:], d_out_weight)


def solution(mesh):
    in_specs = (
        P("rep", "tm", None),
        P(("rep", "tm"), None),
        P(),
        P(),
        P(),
        P(("rep", "tm")),
        P(("rep", "tm")),
        P(("rep", "tm"), None),
    )
    out_specs = (
        P(("rep", "tm"), None),
        P(("rep", "tm"), None),
        P(("rep", "tm"), None),
        P(("rep", "tm"), None),
        P(("rep", "tm"), None),
    )
    return jax.shard_map(shards, mesh=mesh, in_specs=in_specs, out_specs=out_specs, check_vma=False)
```

profile of v0, /device:TPU:0, one launch (start us, length us, event | category | flops | bytes accessed | tf_op | source)
XLA Modules:
  0.0 421.4 jit_solution(12475327256864713558)
XLA Ops:
  7.2 0.0 copy-start
  7.2 0.0 reduce-scatter.5.cloned.1.call-start
  7.2 99.8 %all_to_all.18 = bf16[1024,2,1024]{2,1,0:T(2,128)(2,1)S(1)} all-to-all(bf16[1024,2,1024]{2,1,0:T(2,128)(2,1)} %param.8), channel_id=1, replica_groups=mesh['rep'=2,'tm'=16] {'tm'}, dimensions={0} | all-to-all | bytes 8388608 | tf_op jit(solution)/shard_map/all_to_all | solution.py:81
  107.0 0.0 copy-start.9
  107.0 0.0 copy-start.5
  107.0 0.0 copy-start.6
  107.0 1.3 copy.41
  108.3 0.0 copy-start.2
  108.3 1.9 copy-done.2
  110.3 0.3 fusion.33
  110.6 1.0 copy.42
  111.6 1.1 copy.44
  112.7 1.3 collective-permute-start.1
  114.0 4.3 %collective-permute-start = (bf16[16,32,1024]{2,0,1:T(8,128)(2,1)}, bf16[16,32,1024]{2,0,1:T(8,128)(2,1)}, u32[]{:S(2)}, u32[]{:S(2)}) collective-permute-start(bf16[16,32,1024]{2,0,1:T(8,128)(2,1)} %bitcast.2), channel_id=1, source_target_pairs={{0,1},{1,2},{2,3},{3,4},{4,5},{5,6},{6,7},{7,8},{8,9},{9,10},{10,1... | collective-permute-start | bytes 3145736 | tf_op jit(solution)/shard_map/ppermute | solution.py:16
  118.3 0.0 copy-done.9
  118.3 0.0 copy-done.5
  118.3 2.4 convolution_convert_fusion.4
  120.7 0.2 copy.56
  120.9 0.0 copy-done.6
  120.9 0.2 copy.55
  121.1 0.0 copy-done.7
  121.1 0.1 and_and_fusion
  121.2 0.1 broadcast_in_dim.16
  121.3 0.5 copy.46
  121.8 2.6 copy.43
  124.5 0.0 collective-permute-done.1
  124.5 0.0 collective-permute-done
  124.5 3.0 pad_maximum_fusion.1
  127.5 3.5 copy.45
  131.0 0.0 copy-start.4
  131.0 0.0 copy-done
  131.1 0.0 copy-start.8
  131.1 8.9 %convolution_convert_fusion = bf16[3072,1024]{0,1:T(8,128)(2,1)} fusion(bf16[3072,1024]{1,0:T(8,128)(2,1)S(1)} %bitcast.63, bf16[1024,1024]{1,0:T(8,128)(2,1)S(1)} %copy-done), kind=kOutput, calls=%fused_computation.16 | convolution fusion | flops 6445596672 | bytes 14680064 | tf_op jit(solution)/shard_map/dot_general | solution.py:85
  140.0 0.0 copy-done.4
  140.0 0.0 copy-done.8
  140.0 7.5 %convolution_convert_fusion.1 = bf16[3072,1024]{0,1:T(8,128)(2,1)S(1)} fusion(bf16[3072,1024]{1,0:T(8,128)(2,1)S(1)} %bitcast.64, bf16[1024,1024]{1,0:T(8,128)(2,1)S(1)} %copy-done.8), kind=kOutput, calls=%fused_computation.17 | convolution fusion | flops 6445596672 | bytes 14680064 | tf_op jit(solution)/shard_map/dot_general | solution.py:86
  147.5 0.0 copy-start.3
  147.5 6.3 %fusion.36 = f32[16,64,3072]{2,1,0:T(8,128)} fusion(bf16[64,16,64]{0,2,1:T(8,128)(2,1)S(1)} %bitcast.66, bf16[3072,16,64]{0,2,1:T(8,128)(2,1)S(1)} %bitcast.60), kind=kOutput, calls=%fused_computation.47 | convolution fusion | flops 402653184 | bytes 19005440 | tf_op jit(solution)/shard_map/thd,khd->htk/dot_general | solution.py:62
  153.9 0.0 copy-done.3
  153.9 12.0 %fusion.35 = (f32[16,64]{1,0:T(8,128)S(1)}, f32[16,64,3072]{2,1,0:T(8,128)}) fusion(pred[64,3072]{1,0:T(8,128)(4,1)S(1)} %copy.46, bf16[64,16,64]{0,2,1:T(8,128)(2,1)S(1)} %bitcast.71, bf16[3072,16,64]{0,2,1:T(8,128)(2,1)} %bitcast.74), kind=kOutput, calls=%fused_computation.46 | convolution fusion | flops 415239168 | bytes 19206144 | tf_op jit(solution)/shard_map/sub | solution.py:47
  165.9 8.4 %fusion.20 = bf16[16,64,64]{2,1,0:T(8,128)(2,1)S(1)} fusion(bf16[3072,16,64]{0,2,1:T(8,128)(2,1)} %bitcast.61, f32[16,64,3072]{2,1,0:T(8,128)} %get-tuple-element.32, f32[16,64]{1,0:T(8,128)S(1)} %get-tuple-element.31), kind=kOutput, calls=%fused_computation.25 | convolution fusion | flops 409010176 | bytes 19009536 | tf_op jit(solution)/shard_map/htk,khd->thd/dot_general | solution.py:50
  174.4 1.6 copy-done.10
  175.9 3.7 convert_bitcast_fusion
  179.6 2.1 convolution_convert_fusion.3
  181.7 0.0 reduce-scatter.5.cloned.1.call-update
  181.7 0.0 reduce-scatter.3.cloned.1.call-start
  181.8 22.2 %convert_bitcast_fusion.1 = bf16[3072,16,64]{0,2,1:T(8,128)(2,1)} fusion(bf16[64,16,64]{0,2,1:T(8,128)(2,1)S(1)} %bitcast.72, f32[16,64,3072]{2,1,0:T(8,128)} %fusion.36, f32[16,64,3072]{2,1,0:T(8,128)} %get-tuple-element.32, f32[16,64]{1,0:T(8,128)S(1)} %get-tuple-element.31), kind=kOutput, calls=%fused_computation.11 | convolution fusion | flops 427823104 | bytes 31592448 | tf_op jit(solution)/shard_map/htk,thd->khd/dot_general | solution.py:67
  204.0 15.7 %copy.52 = bf16[3072,16,64]{2,1,0:T(8,128)(2,1)} copy(bf16[3072,16,64]{0,2,1:T(8,128)(2,1)} %convert_bitcast_fusion) | data formatting | bytes 12582912 | tf_op jit(solution)/shard_map/convert_element_type | solution.py:70
  219.7 17.3 %convert_element_type.109 = bf16[96,32,1,1024]{3,1,0,2:T(8,128)(2,1)} reshape(bf16[3072,16,64]{2,1,0:T(8,128)(2,1)} %copy.52) | data formatting | bytes 12582912 | tf_op jit(solution)/shard_map/convert_element_type | solution.py:70
  237.0 15.7 %copy.50 = bf16[3072,16,64]{2,1,0:T(8,128)(2,1)} copy(bf16[3072,16,64]{0,2,1:T(8,128)(2,1)} %convert_bitcast_fusion.1) | data formatting | bytes 12582912 | tf_op jit(solution)/shard_map/convert_element_type | solution.py:68
  252.6 17.3 %convert_element_type.106 = bf16[96,32,1,1024]{3,1,0,2:T(8,128)(2,1)} reshape(bf16[3072,16,64]{2,1,0:T(8,128)(2,1)} %copy.50) | data formatting | bytes 12582912 | tf_op jit(solution)/shard_map/convert_element_type | solution.py:68
  269.9 6.1 %pad_maximum_fusion = bf16[96,32,2,1024]{3,1,0,2:T(8,128)(2,1)S(1)} fusion(bf16[96,32,1,1024]{3,1,0,2:T(8,128)(2,1)} %convert_element_type.109, bf16[96,32,1,1024]{3,1,0,2:T(8,128)(2,1)} %convert_element_type.106), kind=kLoop, calls=%fused_computation.2 | loop fusion | flops 6291456 | bytes 25165824 | tf_op jit(solution)/shard_map/stack | solution.py:103
  276.0 28.3 %copy.53 = bf16[96,32,2,1024]{3,2,1,0:T(2,128)(2,1)S(1)} copy(bf16[96,32,2,1024]{3,1,0,2:T(8,128)(2,1)S(1)} %pad_maximum_fusion) | data formatting | bytes 25165824 | tf_op jit(solution)/shard_map/stack | solution.py:103
  304.3 3.2 copy.57
  307.5 16.2 %convolution_convert_fusion.2 = bf16[1024,2048]{1,0:T(8,128)(2,1)} fusion(bf16[3072,1024]{1,0:T(8,128)(2,1)} %bitcast.65, bf16[3072,2048]{1,0:T(8,128)(2,1)S(1)} %bitcast.62), kind=kOutput, calls=%fused_computation.19 | convolution fusion | flops 12886999040 | bytes 23068672 | tf_op jit(solution)/shard_map/dot_general | solution.py:107
  323.7 0.0 reduce-scatter.3.cloned.1.call-update
  323.7 0.0 copy-start.1
  323.7 21.8 %fusion.17 = bf16[16,64,64]{2,1,0:T(8,128)(2,1)S(1)} fusion(bf16[3072,16,64]{0,2,1:T(8,128)(2,1)} %bitcast.75, f32[16,64,3072]{2,1,0:T(8,128)} %fusion.36, f32[16,64,3072]{2,1,0:T(8,128)} %get-tuple-element.32, f32[16,64]{1,0:T(8,128)S(1)} %get-tuple-element.31), kind=kOutput, calls=%fused_computation.24 | convolution fusion | flops 424742912 | bytes 31592448 | tf_op jit(solution)/shard_map/htk,khd->thd/dot_general | solution.py:65
  345.6 0.8 copy.54
  346.4 2.8 fusion.23
  349.2 1.6 convert_element_type.113
  350.8 61.9 %reduce-scatter.3.cloned.1.call-done = bf16[64,2048]{1,0:T(8,128)(2,1)} async-done(((bf16[1024,2048]{1,0:T(8,128)(2,1)}), bf16[64,2048]{1,0:T(8,128)(2,1)}) %reduce-scatter.3.cloned.1.call-update) | async-done | bytes 262160 | tf_op jit(solution)/shard_map/reduce_scatter | solution.py:106
  412.8 1.8 fusion.34
  414.6 0.0 copy-done.1
  (7 shorter events, 0.0 us)
Async XLA Ops:
  7.2 123.9 %copy-start = (bf16[1024,1024]{1,0:T(8,128)(2,1)S(1)}, bf16[1024,1024]{1,0:T(8,128)(2,1)}, u32[]{:S(2)}) copy-start(bf16[1024,1024]{1,0:T(8,128)(2,1)} %param.10) | copy-start | bytes 6291460
  7.2 342.0 %reduce-scatter.5.cloned.1.call-start = ((), (), s32[]{:S(2)}) async-start(), calls=%async_computation.4 | async-start | bytes 2228224 | tf_op jit(solution)/shard_map/reduce_scatter | solution.py:117
  107.0 11.3 %copy-start.9 = (s32[64]{0:T(128)S(1)}, s32[64]{0:T(128)}, u32[]{:S(2)}) copy-start(s32[64]{0:T(128)} %param.13) | copy-start | bytes 772
  107.0 11.3 %copy-start.5 = (bf16[64,1024]{1,0:T(8,128)(2,1)S(1)}, bf16[64,1024]{1,0:T(8,128)(2,1)}, u32[]{:S(2)}) copy-start(bf16[64,1024]{1,0:T(8,128)(2,1)} %param.15) | copy-start | bytes 393220
  107.0 13.8 %copy-start.6 = (bf16[64,1024]{1,0:T(8,128)(2,1)S(1)}, bf16[64,1024]{1,0:T(8,128)(2,1)}, u32[]{:S(2)}) copy-start(bf16[64,1024]{1,0:T(8,128)(2,1)} %param.9) | copy-start | bytes 393220
  107.0 14.1 %copy-start.7 = (s32[64]{0:T(128)S(1)}, s32[64]{0:T(128)}, u32[]{:S(2)}) copy-start(s32[64]{0:T(128)} %param.14) | copy-start | bytes 772
  108.3 1.9 copy-start.2
  112.7 11.8 %collective-permute-start.1 = (bf16[16,32,1024]{2,0,1:T(8,128)(2,1)}, bf16[16,32,1024]{2,0,1:T(8,128)(2,1)}, u32[]{:S(2)}, u32[]{:S(2)}) collective-permute-start(bf16[16,32,1024]{2,0,1:T(8,128)(2,1)} %bitcast.5), channel_id=1, source_target_pairs={{1,0},{2,1},{3,2},{4,3},{5,4},{6,5},{7,6},{8,7},{9,8},{10,9},{11,1... | collective-permute-start | bytes 3145736 | tf_op jit(solution)/shard_map/ppermute | solution.py:19
  114.0 10.5 %collective-permute-start = (bf16[16,32,1024]{2,0,1:T(8,128)(2,1)}, bf16[16,32,1024]{2,0,1:T(8,128)(2,1)}, u32[]{:S(2)}, u32[]{:S(2)}) collective-permute-start(bf16[16,32,1024]{2,0,1:T(8,128)(2,1)} %bitcast.2), channel_id=1, source_target_pairs={{0,1},{1,2},{2,3},{3,4},{4,5},{5,6},{6,7},{7,8},{8,9},{9,10},{10,1... | collective-permute-start | bytes 3145736 | tf_op jit(solution)/shard_map/ppermute | solution.py:16
  131.0 9.0 %copy-start.4 = (bf16[96,32,1024]{2,1,0:T(8,128)(2,1)}, bf16[96,32,1024]{2,1,0:T(8,128)(2,1)S(1)}, u32[]{:S(2)}) copy-start(bf16[96,32,1024]{2,1,0:T(8,128)(2,1)S(1)} %copy.45) | copy-start | bytes 18874372
  131.1 9.0 %copy-start.8 = (bf16[1024,1024]{1,0:T(8,128)(2,1)S(1)}, bf16[1024,1024]{1,0:T(8,128)(2,1)}, u32[]{:S(2)}) copy-start(bf16[1024,1024]{1,0:T(8,128)(2,1)} %param.11) | copy-start | bytes 6291460
  147.5 6.4 %copy-start.3 = (bf16[3072,1024]{0,1:T(8,128)(2,1)}, bf16[3072,1024]{0,1:T(8,128)(2,1)S(1)}, u32[]{:S(2)}) copy-start(bf16[3072,1024]{0,1:T(8,128)(2,1)S(1)} %convolution_convert_fusion.1) | copy-start | bytes 18874372
  165.9 10.0 %copy-start.10 = (f32[16,64,3072]{2,1,0:T(8,128)S(1)}, f32[16,64,3072]{2,1,0:T(8,128)}, u32[]{:S(2)}) copy-start(f32[16,64,3072]{2,1,0:T(8,128)} %get-tuple-element.32) | copy-start | bytes 37748740
  181.7 231.1 %reduce-scatter.3.cloned.1.call-start = ((), (), s32[]{:S(2)}) async-start(), calls=%async_computation.3 | async-start | bytes 4456448 | tf_op jit(solution)/shard_map/reduce_scatter | solution.py:106
  323.7 90.9 %copy-start.1 = (bf16[1024,1024]{1,0:T(8,128)(2,1)S(1)}, bf16[1024,1024]{1,0:T(8,128)(2,1)}, u32[]{:S(2)}) copy-start(bf16[1024,1024]{1,0:T(8,128)(2,1)} %param.10) | copy-start | bytes 6291460
Sparse Core Ops, SparseCore 0:
  181.8 78.1 reduce-scatter.4
  323.8 88.8 reduce-scatter.2
where the time goes:
time: 423 us; the launch traced here: 421 us
  matrix products  115 us (27%)
  local copies, waits for them, and re-layouts  114 us (27%)
  blocking collectives  99.8 us (24%)
  waiting for transfers between devices  62 us (15%)
  between operations  14.3 us (3%)
  other arithmetic  10.9 us (3%)
  starting transfers between devices  5.67 us (1%)
    all_to_all x1, blocking collectives, shards(): lax.all_to_all(exo_tokens, 'tm', split_axis=0, concat_axis=1, tiled=True)  99.8 us
    reduce_scatter x1, waiting for transfers between devices, shards(): lax.psum_scatter(lax.dot_general(flat_sources, flat_grads, (((0,), (0,)),...  61.9 us
    convert_element_type x2, local copies, waits for them, and re-layouts, attend_block(): value_part = value_part.reshape(n_frames, n_tok, width).astype(jnp.bfloat16)  33 us
    convert_element_type x2, local copies, waits for them, and re-layouts, attend_block(): key_part = key_part.reshape(n_frames, n_tok, width).astype(jnp.bfloat16)  32.9 us
    another operation x1, local copies, waits for them, and re-layouts, shards(): grad_pairs = jnp.stack([key_part, value_part], axis=2)  28.3 us
    dot_general x1, matrix products, attend_block(): jnp.einsum('htk,thd->khd', d_scores, q_heads, preferred_element_type=jnp....  22.2 us
    dot_general x1, matrix products, attend_block(): jnp.einsum('htk,khd->thd', d_scores, k_heads, preferred_element_type=jnp....  21.8 us
    dot_general x1, matrix products, shards(): lax.dot_general(flat_sources, flat_grads, (((0,), (0,)), ((), ())), prefe...  16.2 us
  transfers between devices with their start and end apart: 4, of which 1 were waited for; matrix products, arithmetic and copies ran while one was open for 42% of the time, Pallas kernels for 0%

commit v1 on v0

v1 whole, which is shorter than its diff:
```python
import functools

import jax
import jax.numpy as jnp
from jax import lax
from jax.experimental import pallas as pl
from jax.experimental.pallas import tpu as pltpu
from jax.sharding import PartitionSpec as P

HD = 64
W = 16
QB = 32
GH = 4
GW = GH * HD
LANES = GH * QB
SCALE = HD ** (-0.5)
NEG = -1e30
UNROLL = 4

NT = (((1,), (1,)), ((), ()))
TN = (((0,), (0,)), ((), ()))
NN = (((1,), (0,)), ((), ()))


def dot(a, b, dims):
    return lax.dot_general(a, b, dims, preferred_element_type=jnp.float32)


def spread(rows, head_mask):
    return jnp.concatenate([rows] * GH, axis=0) * head_mask


def fold(wide, head_mask):
    kept = jnp.where(head_mask, wide, 0.0)
    total = kept[0:QB]
    for h in range(1, GH):
        total = total + kept[h * QB : (h + 1) * QB]
    return total


def head_masks():
    row = lax.broadcasted_iota(jnp.int32, (LANES, GW), 0) // QB
    col = lax.broadcasted_iota(jnp.int32, (LANES, GW), 1) // HD
    same = row == col
    return same, jnp.where(same, 1.0, 0.0).astype(jnp.bfloat16)


def window_parts(n_tok):
    n_keys = (QB + 2 * W) * n_tok
    frame = lax.broadcasted_iota(jnp.int32, (n_keys, LANES), 0) // n_tok - W
    query = lax.broadcasted_iota(jnp.int32, (n_keys, LANES), 1) % QB
    return frame, frame - query


def allowed(b, frame, ahead, offsets, total):
    f_abs = frame + b * QB
    return (
        (ahead >= offsets - W) & (ahead <= offsets) & (f_abs >= 0) & (f_abs < total)
    )


def stats_kernel(n_tok, total, q_ref, d_ref, k_ref, v_ref, off_ref, m_ref, l_ref, s_ref):
    _, mask_b = head_masks()
    frame, ahead = window_parts(n_tok)
    n_keys = frame.shape[0]

    def step(b, carry):
        rows = pl.ds(pl.multiple_of(b * QB, QB), QB)
        keys = pl.ds(pl.multiple_of(b * QB * n_tok, QB * n_tok), n_keys)
        q4 = spread(q_ref[rows, :], mask_b)
        d4 = spread(d_ref[rows, :], mask_b)
        allow = allowed(b, frame, ahead, off_ref[pl.ds(b, 1), :], total)
        scores = jnp.where(allow, dot(k_ref[keys, :], q4, NT) * SCALE, NEG)
        top = jnp.max(scores, axis=0, keepdims=True)
        expo = jnp.exp(scores - top)
        d_probs = dot(v_ref[keys, :], d4, NT)
        m_ref[0, pl.ds(b, 1), :] = top
        l_ref[0, pl.ds(b, 1), :] = jnp.sum(expo, axis=0, keepdims=True)
        s_ref[0, pl.ds(b, 1), :] = jnp.sum(expo * d_probs, axis=0, keepdims=True)
        return carry

    lax.fori_loop(0, total // QB, step, 0, unroll=UNROLL)


def value_kernel(
    n_tok, total, q_ref, d_ref, k_ref, v_ref, off_ref, m_ref, l_ref, o_ref, g_ref, acc, ctx
):
    same, mask_b = head_masks()
    frame, ahead = window_parts(n_tok)
    n_keys = frame.shape[0]
    acc[...] = jnp.zeros_like(acc)

    def step(b, carry):
        rows = pl.ds(pl.multiple_of(b * QB, QB), QB)
        keys = pl.ds(pl.multiple_of(b * QB * n_tok, QB * n_tok), n_keys)
        q4 = spread(q_ref[rows, :], mask_b)
        d4 = spread(d_ref[rows, :], mask_b)
        allow = allowed(b, frame, ahead, off_ref[pl.ds(b, 1), :], total)
        scores = jnp.where(allow, dot(k_ref[keys, :], q4, NT) * SCALE, NEG)
        probs = jnp.exp(scores - m_ref[0, pl.ds(b, 1), :]) * l_ref[0, pl.ds(b, 1), :]
        probs_b = probs.astype(jnp.bfloat16)
        ctx[rows, :] = fold(dot(probs_b, v_ref[keys, :], TN), same)
        acc[keys, :] += dot(probs_b, d4, NN)
        return carry

    lax.fori_loop(0, total // QB, step, 0, unroll=UNROLL)
    o_ref[...] = ctx[...].T.astype(jnp.bfloat16)
    g_ref[...] = acc[...].astype(jnp.bfloat16)


def key_kernel(
    n_tok, total, q_ref, d_ref, k_ref, v_ref, off_ref, m_ref, l_ref, s_ref, dq_ref, g_ref, acc
):
    same, mask_b = head_masks()
    frame, ahead = window_parts(n_tok)
    n_keys = frame.shape[0]
    acc[...] = jnp.zeros_like(acc)

    def step(b, carry):
        rows = pl.ds(pl.multiple_of(b * QB, QB), QB)
        keys = pl.ds(pl.multiple_of(b * QB * n_tok, QB * n_tok), n_keys)
        q4 = spread(q_ref[rows, :], mask_b)
        d4 = spread(d_ref[rows, :], mask_b)
        allow = allowed(b, frame, ahead, off_ref[pl.ds(b, 1), :], total)
        k_blk = k_ref[keys, :]
        scores = jnp.where(allow, dot(k_blk, q4, NT) * SCALE, NEG)
        probs = jnp.exp(scores - m_ref[0, pl.ds(b, 1), :]) * l_ref[0, pl.ds(b, 1), :]
        d_probs = dot(v_ref[keys, :], d4, NT)
        d_scores = probs * (d_probs - s_ref[0, pl.ds(b, 1), :]) * SCALE
        d_scores = d_scores.astype(jnp.bfloat16)
        dq_ref[rows, :] = fold(dot(d_scores, k_blk, TN), same).astype(jnp.bfloat16)
        acc[keys, :] += dot(d_scores, q4, NN)
        return carry

    lax.fori_loop(0, total // QB, step, 0, unroll=UNROLL)
    g_ref[...] = acc[...].astype(jnp.bfloat16)


def attention_calls(n_tok, total, width):
    groups = width // GW
    blocks = total // QB
    key_rows = (total + 2 * W) * n_tok
    by_query = pl.BlockSpec((total, GW), lambda g: (0, g))
    by_key = pl.BlockSpec((key_rows, GW), lambda g: (0, g))
    by_offset = pl.BlockSpec((blocks, LANES), lambda g: (0, 0))
    by_stat = pl.BlockSpec((1, blocks, LANES), lambda g: (g, 0, 0))
    by_feature = pl.BlockSpec((GW, total), lambda g: (g, 0))
    stat = jax.ShapeDtypeStruct((groups, blocks, LANES), jnp.float32)
    key_like = jax.ShapeDtypeStruct((key_rows, width), jnp.bfloat16)
    key_acc = pltpu.VMEM((key_rows, GW), jnp.float32)
    params = pltpu.CompilerParams(vmem_limit_bytes=48 * 1024 * 1024)
    unit = 2 * groups * blocks * (QB + 2 * W) * n_tok * LANES * GW
    common = [by_query, by_query, by_key, by_key, by_offset]

    def cost(dots):
        return pl.CostEstimate(
            flops=4 * dots * unit, bytes_accessed=8 * key_rows * width, transcendentals=0
        )

    stats = pl.pallas_call(
        functools.partial(stats_kernel, n_tok, total),
        grid=(groups,),
        in_specs=common,
        out_specs=[by_stat] * 3,
        out_shape=[stat] * 3,
        compiler_params=params,
        cost_estimate=cost(2),
        name="softmax_stats",
    )
    value = pl.pallas_call(
        functools.partial(value_kernel, n_tok, total),
        grid=(groups,),
        in_specs=common + [by_stat] * 2,
        out_specs=[by_feature, by_key],
        out_shape=[jax.ShapeDtypeStruct((width, total), jnp.bfloat16), key_like],
        scratch_shapes=[key_acc, pltpu.VMEM((total, GW), jnp.float32)],
        compiler_params=params,
        cost_estimate=cost(3),
        name="context_and_value_part",
    )
    key = pl.pallas_call(
        functools.partial(key_kernel, n_tok, total),
        grid=(groups,),
        in_specs=common + [by_stat] * 3,
        out_specs=[by_query, by_key],
        out_shape=[jax.ShapeDtypeStruct((total, width), jnp.bfloat16), key_like],
        scratch_shapes=[key_acc],
        compiler_params=params,
        cost_estimate=cost(4),
        name="query_and_key_part",
    )
    return stats, value, key


def shards(
    exo_tokens, queries, key_weight, value_weight, out_weight, gaze_valid, window_offset, cotangent
):
    rows_here = queries.shape[0]
    width = queries.shape[1]
    total = rows_here * lax.axis_size("tm")
    n_tok = exo_tokens.shape[1]
    blocks = total // QB
    valid_col = gaze_valid.astype(jnp.float32)[:, None]
    masked_grad = (cotangent.astype(jnp.float32) * valid_col).astype(jnp.bfloat16)
    extra = jnp.broadcast_to(window_offset.astype(jnp.bfloat16)[:, None], (rows_here, 128))
    q_all = lax.all_gather(queries, "tm", axis=0, tiled=True)
    grad_all = lax.all_gather(
        jnp.concatenate([masked_grad, extra], axis=1), "tm", axis=0, tiled=True
    )
    offsets = grad_all[:, width].astype(jnp.int32).reshape(blocks, 1, QB)
    offsets = jnp.broadcast_to(offsets, (blocks, GH, QB)).reshape(blocks, LANES)
    grad_all = grad_all[:, :width]

    flat = exo_tokens.reshape(-1, width)
    flat = jnp.pad(flat, ((W * n_tok, W * n_tok), (0, 0)))
    keys = dot(flat, key_weight, NN).astype(jnp.bfloat16)
    values = dot(flat, value_weight, NN).astype(jnp.bfloat16)
    d_context = dot(grad_all, out_weight, NT).astype(jnp.bfloat16)

    stats_call, value_call, key_call = attention_calls(n_tok, total, width)
    common = (q_all, d_context, keys, values, offsets)
    top, norm, slope = stats_call(*common)
    top_all = lax.pmax(top, "tm")
    factor = jnp.exp(top - top_all)
    sums = lax.psum(jnp.stack([norm * factor, slope * factor]), "tm")
    inverse = 1.0 / sums[0]
    slope_all = sums[1] * inverse

    context_t, value_part = value_call(*common, top_all, inverse)
    context_t = lax.psum_scatter(context_t, "tm", scatter_dimension=0, tiled=True)
    value_term = dot(flat, value_part, TN).astype(jnp.bfloat16)
    d_value = lax.psum_scatter(value_term, "tm", scatter_dimension=0, tiled=True)

    d_query, key_part = key_call(*common, top_all, inverse, slope_all)
    d_query = lax.psum_scatter(d_query, "tm", scatter_dimension=0, tiled=True)
    key_term = dot(flat, key_part, TN).astype(jnp.bfloat16)
    d_key = lax.psum_scatter(key_term, "tm", scatter_dimension=0, tiled=True)

    d_out = dot(context_t, grad_all, NN)
    context = lax.all_to_all(context_t, "tm", split_axis=1, concat_axis=0, tiled=True)
    attended = (dot(context, out_weight, TN) * valid_col).astype(jnp.bfloat16)
    return (
        attended,
        d_query,
        d_key.astype(jnp.float32),
        d_value.astype(jnp.float32),
        d_out,
    )


def solution(mesh):
    in_specs = (
        P("rep", "tm", None),
        P(("rep", "tm"), None),
        P(),
        P(),
        P(),
        P(("rep", "tm")),
        P(("rep", "tm")),
        P(("rep", "tm"), None),
    )
    out_specs = (P(("rep", "tm"), None),) * 5
    return jax.shard_map(shards, mesh=mesh, in_specs=in_specs, out_specs=out_specs, check_vma=False)
```

time: 423 us -> 597 us (1.41)
  waiting for transfers between devices: 62 us -> 413 us
  blocking collectives: 99.8 us -> 0 us
  local copies, waits for them, and re-layouts: 114 us -> 20 us
  Pallas kernels: 0 us -> 89.4 us
  matrix products: 115 us -> 44.1 us
    reduce_scatter x2 -> x4, waiting for transfers between devices: 62 us -> 180 us  [the longest x1 62.7 us: shards(): lax.psum_scatter(value_term, 'tm', scatter_dimension=0, tiled=True)]
    all_to_all x1 -> x0, blocking collectives: 99.8 us -> none  [shards(): lax.all_to_all(exo_tokens, 'tm', split_axis=0, concat_axis=1, tiled=True)]
    psum x0 -> x1, waiting for transfers between devices: none -> 90.8 us  [shards(): sums = lax.psum(jnp.stack([norm * factor, slope * factor]), 'tm')]
    pallas_call x0 -> x3, Pallas kernels: none -> 89.4 us  [the longest x1 40.1 us: shards(): d_query, key_part = key_call(*common, top_all, inverse, slope_all)]
    pmax x0 -> x1, waiting for transfers between devices: none -> 83.4 us  [shards(): top_all = lax.pmax(top, 'tm')]
    convert_element_type x4 -> x1, local copies, waits for them, and re-layouts: 65.9 us -> 0.07 us  [shards(): offsets = grad_all[:, width].astype(jnp.int32).reshape(blocks, 1, QB)]
    dot_general x11 -> x7, matrix products: 102 us -> 44.1 us  [dot(): return lax.dot_general(a, b, dims, preferred_element_type=jnp.float32)]
    all_gather x0 -> x2, waiting for transfers between devices: none -> 57.6 us  [the longest x1 35.1 us: shards(): q_all = lax.all_gather(queries, 'tm', axis=0, tiled=True)]
  transfers between devices with their start and end apart: 4 -> 9, of which waited for: 1 -> 8; matrix products, arithmetic and copies ran while one was open for 42% -> 10% of each run, Pallas kernels for 0% -> 7%
where the time goes in v1:
time: 597 us; the launch traced here: 596 us
  waiting for transfers between devices  413 us (69%)
  Pallas kernels  89.4 us (15%)
  matrix products  44.1 us (7%)
  local copies, waits for them, and re-layouts  20 us (3%)
  between operations  14.3 us (2%)
  other arithmetic  9.96 us (2%)
    psum x1, waiting for transfers between devices, shards(): sums = lax.psum(jnp.stack([norm * factor, slope * factor]), 'tm')  90.8 us
    pmax x1, waiting for transfers between devices, shards(): top_all = lax.pmax(top, 'tm')  83.4 us
    reduce_scatter x1, waiting for transfers between devices, shards(): lax.psum_scatter(value_term, 'tm', scatter_dimension=0, tiled=True)  62.7 us
    reduce_scatter x1, waiting for transfers between devices, shards(): d_key = lax.psum_scatter(key_term, 'tm', scatter_dimension=0, tiled=True)  57.8 us
    reduce_scatter x1, waiting for transfers between devices, shards(): d_query = lax.psum_scatter(d_query, 'tm', scatter_dimension=0, tiled=True)  57.5 us
    dot_general x7, matrix products, dot(): return lax.dot_general(a, b, dims, preferred_element_type=jnp.float32)  44.1 us
    pallas_call x1, Pallas kernels, shards(): d_query, key_part = key_call(*common, top_all, inverse, slope_all)  40.1 us
    all_gather x1, waiting for transfers between devices, shards(): q_all = lax.all_gather(queries, 'tm', axis=0, tiled=True)  35.1 us
  transfers between devices with their start and end apart: 9, of which 8 were waited for; matrix products, arithmetic and copies ran while one was open for 10% of the time, Pallas kernels for 7%

profile of v1, /device:TPU:0, one launch (start us, length us, event | category | flops | bytes accessed | tf_op | source)
XLA Modules:
  0.0 595.9 jit_solution(15661550091842786263)
XLA Ops:
  7.2 0.0 copy-start
  7.2 0.0 all-gather.5.cloned.1.call-start
  7.2 0.8 convert_element_type.49
  8.0 0.7 convert_element_type.51
  8.7 1.0 multiply_convert_fusion
  9.7 0.1 broadcast_in_dim.4
  9.8 0.7 pad_maximum_fusion
  10.4 0.0 all-gather.5.cloned.1.call-update
  10.5 0.0 all-gather.3.cloned.1.call-start
  10.5 0.7 all-gather.3.cloned.1.call-update
  11.2 0.0 all-reduce.4.cloned.1.call-start
  11.3 7.2 %reshape.31 = bf16[2048,1024]{1,0:T(8,128)(2,1)} reshape(bf16[1024,2,1024]{2,1,0:T(2,128)(2,1)} %param.8) | data formatting | bytes 8388608 | tf_op jit(solution)/shard_map/reshape | solution.py:214
  18.5 8.6 %convolution_convert_fusion.v_ref = bf16[2112,1024]{1,0:T(8,128)(2,1)} fusion(bf16[1024,1024]{1,0:T(8,128)(2,1)S(1)} %copy-done, bf16[2048,1024]{1,0:T(8,128)(2,1)} %reshape.31), kind=kOutput, calls=%fused_computation | convolution fusion | flops 4431347712 | bytes 10616832 | tf_op jit(solution)/shard_map/dot_general | solution.py:26
  27.1 6.3 %convolution_convert_fusion.1.k_ref = bf16[2112,1024]{1,0:T(8,128)(2,1)} fusion(bf16[1024,1024]{1,0:T(8,128)(2,1)S(1)} %copy-done.12, bf16[2048,1024]{1,0:T(8,128)(2,1)S(1)} %copy-done.9), kind=kOutput, calls=%fused_computation.1 | convolution fusion | flops 4431347712 | bytes 10616832 | tf_op jit(solution)/shard_map/dot_general | solution.py:26
  33.4 22.5 %all-gather.5.cloned.1.call-done = bf16[1024,1152]{1,0:T(8,128)(2,1)} async-done(((bf16[64,1152]{1,0:T(8,128)(2,1)}), bf16[1024,1152]{1,0:T(8,128)(2,1)}) %all-gather.5.cloned.1.call-update) | async-done | bytes 2359312 | tf_op jit(solution)/shard_map/all_gather | solution.py:207
  55.8 1.2 convert_reduce_fusion
  57.0 0.1 reshape.33
  57.1 0.1 reshape.32.off_ref
  57.2 5.9 convolution_convert_fusion.2.d_ref
  63.1 35.1 %all-gather.3.cloned.1.call-done.q_ref = bf16[1024,1024]{1,0:T(8,128)(2,1)} async-done(((bf16[64,1024]{1,0:T(8,128)(2,1)}), bf16[1024,1024]{1,0:T(8,128)(2,1)}) %all-gather.3.cloned.1.call-update) | async-done | bytes 2097168 | tf_op jit(solution)/shard_map/all_gather | solution.py:206
  98.2 1.6 copy-done.5
  99.8 1.6 copy-done.8
  101.4 14.4 %softmax_stats.1 = (f32[4,32,128]{2,1,0:T(8,128)}, f32[4,32,128]{2,1,0:T(8,128)S(1)}, f32[4,32,128]{2,1,0:T(8,128)S(1)}) custom-call(bf16[1024,1024]{1,0:T(8,128)(2,1)S(1)} %copy-done.5, bf16[1024,1024]{1,0:T(8,128)(2,1)S(1)} %copy-done.8, bf16[2112,1024]{1,0:T(8,128)(2,1)} %convolution_convert_fusion.1.k_ref, ...), custom_call_target="tpu_custom_call" | custom-call | flops 8589934592 | bytes 17301504 | tf_op jit(solution)/shard_map/softmax_stats/pallas_call | solution.py:222
  115.8 0.0 all-reduce.4.cloned.1.call-update
  115.8 0.0 all-reduce.6.cloned.1.call-start
  115.9 83.4 %all-reduce.4.cloned.1.call-done.m_ref = f32[4,32,128]{2,1,0:T(8,128)} async-done(((f32[4,32,128]{2,1,0:T(8,128)}), f32[4,32,128]{2,1,0:T(8,128)}) %all-reduce.4.cloned.1.call-update) | async-done | bytes 65552 | tf_op jit(solution)/shard_map/pmax | solution.py:223
  199.3 0.9 multiply_bitcast_fusion.1
  200.2 0.7 pad_maximum_fusion.1
  200.9 0.0 all-reduce.6.cloned.1.call-update
  200.9 0.0 reduce-scatter.5.cloned.1.call-start
  201.0 90.8 %all-reduce.6.cloned.1.call-done = f32[2,4,32,128]{3,2,1,0:T(8,128)} async-done(((f32[2,4,32,128]{3,2,1,0:T(8,128)}), f32[2,4,32,128]{3,2,1,0:T(8,128)}) %all-reduce.6.cloned.1.call-update) | async-done | bytes 131088 | tf_op jit(solution)/shard_map/psum | solution.py:225
  291.7 0.9 fusion.17.l_ref
  292.6 0.0 copy-start.3
  292.6 0.8 copy-done.3
  293.4 1.6 copy-done.6
  295.0 34.9 %context_and_value_part.1 = (bf16[1024,1024]{1,0:T(8,128)(2,1)S(1)}, bf16[2112,1024]{1,0:T(8,128)(2,1)}) custom-call(bf16[1024,1024]{1,0:T(8,128)(2,1)S(1)} %copy-done.6, bf16[1024,1024]{1,0:T(8,128)(2,1)} %convolution_convert_fusion.2.d_ref, bf16[2112,1024]{1,0:T(8,128)(2,1)} %convolution_convert_fusion.1.k_ref, ...), custom_call_target="tpu_custom_call" | custom-call | flops 12884901888 | bytes 17301504 | tf_op jit(solution)/shard_map/context_and_value_part/pallas_call | solution.py:229
  329.9 1.4 copy-done.2
  331.3 0.0 reduce-scatter.5.cloned.1.call-update
  331.3 0.0 reduce-scatter.9.cloned.1.call-start
  331.4 1.6 copy-done.7
  333.0 40.1 %query_and_key_part.1 = (bf16[1024,1024]{1,0:T(8,128)(2,1)S(1)}, bf16[2112,1024]{1,0:T(8,128)(2,1)}) custom-call(bf16[1024,1024]{1,0:T(8,128)(2,1)S(1)} %copy-done.7, bf16[1024,1024]{1,0:T(8,128)(2,1)} %convolution_convert_fusion.2.d_ref, bf16[2112,1024]{1,0:T(8,128)(2,1)} %convolution_convert_fusion.1.k_ref, ...), custom_call_target="tpu_custom_call" | custom-call | flops 17179869184 | bytes 17301504 | tf_op jit(solution)/shard_map/query_and_key_part/pallas_call | solution.py:234
  373.1 1.4 copy-done.1
  374.4 8.6 %fusion.6 = bf16[1024,1024]{1,0:T(8,128)(2,1)} fusion(bf16[2112,1024]{1,0:T(8,128)(2,1)} %get-tuple-element.17, bf16[2048,1024]{1,0:T(8,128)(2,1)S(1)} %copy-done.10), kind=kOutput, calls=%fused_computation.8 | convolution fusion | flops 4430233600 | bytes 10616832 | tf_op jit(solution)/shard_map/dot_general | solution.py:26
  383.1 0.0 reduce-scatter.9.cloned.1.call-update
  383.1 0.2 reduce-scatter.11.cloned.1.call-start
  383.3 9.1 %fusion.9 = bf16[1024,1024]{1,0:T(8,128)(2,1)} fusion(bf16[2112,1024]{1,0:T(8,128)(2,1)} %get-tuple-element.18, bf16[2048,1024]{1,0:T(8,128)(2,1)} %reshape.31), kind=kOutput, calls=%fused_computation.9 | convolution fusion | flops 4430233600 | bytes 10616832 | tf_op jit(solution)/shard_map/dot_general | solution.py:26
  392.4 0.0 reduce-scatter.11.cloned.1.call-update
  392.5 0.0 reduce-scatter.7.cloned.1.call-start
  392.5 0.7 reduce-scatter.7.cloned.1.call-update
  393.2 1.6 reduce-scatter.5.cloned.1.call-done
  394.8 1.1 copy.16
  395.9 0.9 reshape.35
  396.8 4.8 all-to-all-start
  401.6 57.8 %reduce-scatter.9.cloned.1.call-done = bf16[64,1024]{1,0:T(8,128)(2,1)} async-done(((bf16[1024,1024]{1,0:T(8,128)(2,1)}), bf16[64,1024]{1,0:T(8,128)(2,1)}) %reduce-scatter.9.cloned.1.call-update) | async-done | bytes 131088 | tf_op jit(solution)/shard_map/reduce_scatter | solution.py:237
  459.4 1.6 convert_element_type.59
  461.0 62.7 %reduce-scatter.11.cloned.1.call-done = bf16[64,1024]{1,0:T(8,128)(2,1)} async-done(((bf16[1024,1024]{1,0:T(8,128)(2,1)}), bf16[64,1024]{1,0:T(8,128)(2,1)}) %reduce-scatter.11.cloned.1.call-update) | async-done | bytes 131088 | tf_op jit(solution)/shard_map/reduce_scatter | solution.py:232
  523.7 1.6 convert_element_type.61
  525.3 2.9 fusion.12
  528.2 0.0 all-to-all-done
  528.2 0.2 reshape.36
  528.4 0.2 copy.15
  528.6 0.2 all_to_all.17
  528.8 2.7 fusion.15
  531.5 57.5 %reduce-scatter.7.cloned.1.call-done = bf16[64,1024]{1,0:T(8,128)(2,1)} async-done(((bf16[1024,1024]{1,0:T(8,128)(2,1)}), bf16[64,1024]{1,0:T(8,128)(2,1)}) %reduce-scatter.7.cloned.1.call-update) | async-done | bytes 131088 | tf_op jit(solution)/shard_map/reduce_scatter | solution.py:235
  (20 shorter events, 0.1 us)
Async XLA Ops:
  7.2 11.3 %copy-start = (bf16[1024,1024]{1,0:T(8,128)(2,1)S(1)}, bf16[1024,1024]{1,0:T(8,128)(2,1)}, u32[]{:S(2)}) copy-start(bf16[1024,1024]{1,0:T(8,128)(2,1)} %param.11) | copy-start | bytes 6291460
  7.2 48.6 %all-gather.5.cloned.1.call-start = ((), (), s32[]{:S(2)}) async-start(), calls=%async_computation.6 | async-start | bytes 2506752 | tf_op jit(solution)/shard_map/all_gather | solution.py:207
  10.5 87.7 %all-gather.3.cloned.1.call-start = ((), (), s32[]{:S(2)}) async-start(), calls=%async_computation.5 | async-start | bytes 2228224 | tf_op jit(solution)/shard_map/all_gather | solution.py:206
  11.2 188.1 %all-reduce.4.cloned.1.call-start = ((), (), s32[]{:S(2)}) async-start(), calls=%async_computation.7 | async-start | bytes 131072 | tf_op jit(solution)/shard_map/pmax | solution.py:223
  18.5 8.6 %copy-start.9 = (bf16[2048,1024]{1,0:T(8,128)(2,1)S(1)}, bf16[2048,1024]{1,0:T(8,128)(2,1)}, u32[]{:S(2)}) copy-start(bf16[2048,1024]{1,0:T(8,128)(2,1)} %reshape.31) | copy-start | bytes 12582916
  18.5 8.6 %copy-start.12 = (bf16[1024,1024]{1,0:T(8,128)(2,1)S(1)}, bf16[1024,1024]{1,0:T(8,128)(2,1)}, u32[]{:S(2)}) copy-start(bf16[1024,1024]{1,0:T(8,128)(2,1)} %param.10) | copy-start | bytes 6291460
  98.2 1.6 copy-start.5
  99.8 1.6 copy-start.8
  115.8 175.9 %all-reduce.6.cloned.1.call-start = ((), (), s32[]{:S(2)}) async-start(), calls=%async_computation.8 | async-start | bytes 262144 | tf_op jit(solution)/shard_map/psum | solution.py:225
  200.9 193.9 %reduce-scatter.5.cloned.1.call-start = ((), (), s32[]{:S(2)}) async-start(), calls=%async_computation.9 | async-start | bytes 2228224 | tf_op jit(solution)/shard_map/reduce_scatter | solution.py:230
  292.6 0.8 copy-start.3
  293.4 1.6 copy-start.6
  295.0 36.4 %copy-start.11 = (f32[2,4,32,128]{3,2,1,0:T(8,128)S(1)}, f32[2,4,32,128]{3,2,1,0:T(8,128)}, u32[]{:S(2)}) copy-start(f32[2,4,32,128]{3,2,1,0:T(8,128)} %all-reduce.6.cloned.1.call-done) | copy-start | bytes 393220
  295.0 36.4 %copy-start.4 = (f32[4,32,128]{2,1,0:T(8,128)S(1)}, f32[4,32,128]{2,1,0:T(8,128)}, u32[]{:S(2)}) copy-start(f32[4,32,128]{2,1,0:T(8,128)} %all-reduce.4.cloned.1.call-done.m_ref) | copy-start | bytes 196612
  329.9 1.4 copy-start.2
  331.3 128.1 %reduce-scatter.9.cloned.1.call-start = ((), (), s32[]{:S(2)}) async-start(), calls=%async_computation.11 | async-start | bytes 2228224 | tf_op jit(solution)/shard_map/reduce_scatter | solution.py:237
  331.4 1.6 copy-start.7
  333.0 41.4 %copy-start.10 = (bf16[2048,1024]{1,0:T(8,128)(2,1)S(1)}, bf16[2048,1024]{1,0:T(8,128)(2,1)}, u32[]{:S(2)}) copy-start(bf16[2048,1024]{1,0:T(8,128)(2,1)} %reshape.31) | copy-start | bytes 12582916
  373.1 1.4 copy-start.1
  383.1 140.6 %reduce-scatter.11.cloned.1.call-start = ((), (), s32[]{:S(2)}) async-start(), calls=%async_computation.12 | async-start | bytes 2228224 | tf_op jit(solution)/shard_map/reduce_scatter | solution.py:232
  392.5 196.5 %reduce-scatter.7.cloned.1.call-start = ((), (), s32[]{:S(2)}) async-start(), calls=%async_computation.10 | async-start | bytes 2228224 | tf_op jit(solution)/shard_map/reduce_scatter | solution.py:235
  396.8 131.4 %all-to-all-start = ((bf16[16,2,2048]{2,1,0:T(2,128)(2,1)}), bf16[16,2,2048]{2,1,0:T(2,128)(2,1)S(1)}, u32[]{:S(2)}, u32[]{:S(2)}) async-start(bf16[16,2,2048]{2,1,0:T(2,128)(2,1)} %reshape.35), calls=%async_computation.1 | async-start | bytes 262144 | tf_op jit(solution)/shard_map/all_to_all | solution.py:240
Sparse Core Ops, SparseCore 0:
  10.9 44.9 all-gather.4
  58.0 40.1 all-gather.2
  116.0 83.3 all-reduce.3
  203.2 88.4 all-reduce.5
  331.4 63.3 reduce-scatter.4
  398.9 60.4 reduce-scatter.8
  463.1 60.5 reduce-scatter.10
  528.5 60.4 reduce-scatter.6

commit v2 on v1

v2 whole, which is shorter than its diff:
```python
import functools
import itertools

import jax
import jax.numpy as jnp
from jax import lax
from jax.experimental import pallas as pl
from jax.experimental.pallas import tpu as pltpu
from jax.sharding import PartitionSpec as P

HD = 64
W = 16
QB = 32
GH = 4
GW = GH * HD
LANES = GH * QB
SCALE = HD ** (-0.5)
NEG = -1e30
UNROLL = 4

NT = (((1,), (1,)), ((), ()))
TN = (((0,), (0,)), ((), ()))
NN = (((1,), (0,)), ((), ()))


def dot(a, b, dims):
    return lax.dot_general(a, b, dims, preferred_element_type=jnp.float32)


def spread(rows, head_mask):
    return jnp.concatenate([rows] * GH, axis=0) * head_mask


def fold(wide, head_mask):
    kept = jnp.where(head_mask, wide, 0.0)
    total = kept[0:QB]
    for h in range(1, GH):
        total = total + kept[h * QB : (h + 1) * QB]
    return total


def head_masks():
    row = lax.broadcasted_iota(jnp.int32, (LANES, GW), 0) // QB
    col = lax.broadcasted_iota(jnp.int32, (LANES, GW), 1) // HD
    same = row == col
    return same, jnp.where(same, 1.0, 0.0).astype(jnp.bfloat16)


def window_parts(n_tok):
    n_keys = (QB + 2 * W) * n_tok
    frame = lax.broadcasted_iota(jnp.int32, (n_keys, LANES), 0) // n_tok - W
    query = lax.broadcasted_iota(jnp.int32, (n_keys, LANES), 1) % QB
    return frame, frame - query


def allowed(b, frame, ahead, offsets, total):
    f_abs = frame + b * QB
    return (
        (ahead >= offsets - W) & (ahead <= offsets) & (f_abs >= 0) & (f_abs < total)
    )


def bit_of(me, k):
    return lax.rem(me // (1 << k), 2)


def partner_of(me, k):
    return me + (1 << k) * (1 - 2 * bit_of(me, k))


def greet(others):
    barrier = pltpu.get_barrier_semaphore()
    for other in others:
        pl.semaphore_signal(
            barrier, inc=1, device_id={"tm": other}, device_id_type=pl.DeviceIdType.MESH
        )
    pl.semaphore_wait(barrier, len(others))


def remote(src, dst, send, recv, other):
    return pltpu.make_async_remote_copy(
        src_ref=src,
        dst_ref=dst,
        send_sem=send,
        recv_sem=recv,
        device_id={"tm": other},
        device_id_type=pl.DeviceIdType.MESH,
    )


def at_bits(ref, bits, chosen):
    return ref.at[tuple(chosen[k] if k in chosen else slice(None) for k in bits)]


class Gather:
    def __init__(self, me, n_bits, order, out, send, recv):
        self.me, self.order, self.out = me, order, out
        self.bits = list(range(n_bits))[::-1]
        self.send, self.recv = send, recv

    def copy(self, step):
        held = {k: bit_of(self.me, k) for k in self.order[step:]}
        part = at_bits(self.out, self.bits, held)
        other = partner_of(self.me, self.order[step])
        return remote(part, part, self.send.at[step], self.recv.at[step], other)


class Reduce:
    def __init__(self, me, n_bits, order, src, slots, send, recv):
        self.me, self.order = me, order
        self.bits = list(range(n_bits))[::-1]
        self.refs = [src] + list(slots)
        self.send, self.recv = send, recv

    def left(self, step):
        return [k for k in self.bits if k not in self.order[:step]]

    def copy(self, step):
        k = self.order[step]
        part = at_bits(self.refs[step], self.left(step), {k: 1 - bit_of(self.me, k)})
        other = partner_of(self.me, k)
        return remote(part, self.refs[step + 1], self.send.at[step], self.recv.at[step], other)

    def finish(self, step):
        self.copy(step).wait()
        k = self.order[step]
        bits = self.left(step)
        rest = [other for other in bits if other != k]
        for index in itertools.product((0, 1), repeat=len(rest)):
            chosen = dict(zip(rest, index))
            chosen[k] = bit_of(self.me, k)
            own = self.refs[step][tuple(chosen[bit] for bit in bits)]
            got = self.refs[step + 1][index]
            total = own.astype(jnp.float32) + got.astype(jnp.float32)
            self.refs[step + 1][index] = total.astype(jnp.bfloat16)


def slot_shapes(n_bits, rows, width):
    return [
        pltpu.VMEM((2,) * (n_bits - 1 - step) + (rows, width), jnp.bfloat16)
        for step in range(n_bits)
    ]


def low_first(n_bits):
    return list(range(n_bits))


def late_one(n_bits):
    return [0] + list(range(2, n_bits)) + [1]


def project_kernel(
    n_bits, chunk, q_ref, g_ref, x_ref, kw_ref, vw_ref, qo_ref, go_ref, k_ref, v_ref, send, recv
):
    me = lax.axis_index("tm")
    greet([partner_of(me, k) for k in range(n_bits)])
    orders = (list(range(1, n_bits))[::-1] + [0], [1] + list(range(2, n_bits))[::-1] + [0])
    gathers = []
    for i, (mine, out) in enumerate(((q_ref, qo_ref), (g_ref, go_ref))):
        out[tuple(bit_of(me, k) for k in range(n_bits)[::-1])] = mine[...]
        gathers.append(Gather(me, n_bits, orders[i], out, send.at[i], recv.at[i]))
    for gather in gathers:
        gather.copy(0).start()
    rows, width = x_ref.shape
    n_cols = width // GW

    def piece(j, carry):
        cols = pl.ds(pl.multiple_of(j * GW, GW), GW)

        def part(i, inner):
            here = pl.ds(pl.multiple_of(i * chunk, 16), chunk)
            x = x_ref[here, :]
            k_ref[here, cols] = dot(x, kw_ref[:, cols], NN).astype(jnp.bfloat16)
            v_ref[here, cols] = dot(x, vw_ref[:, cols], NN).astype(jnp.bfloat16)
            return inner

        lax.fori_loop(0, rows // chunk, part, 0)
        return carry

    for step in range(n_bits):
        lax.fori_loop(n_cols * step // n_bits, n_cols * (step + 1) // n_bits, piece, 0)
        for gather in gathers:
            gather.copy(step).wait()
            if step + 1 < n_bits:
                gather.copy(step + 1).start()


def place(b, per, groups, g):
    return b // per, pl.ds(lax.rem(b, per) * groups + g, 1)


def stats_kernel(
    n_tok, total, n_dev, q_ref, d_ref, k_ref, v_ref, off_ref, res_ref, mine, got, out_ref,
    send, recv, send_back, recv_back,
):
    _, mask_b = head_masks()
    frame, ahead = window_parts(n_tok)
    n_keys = frame.shape[0]
    g = pl.program_id(0)
    groups = pl.num_programs(0)
    per = total // QB // n_dev
    me = lax.axis_index("tm")

    @pl.when(g == 0)
    def _():
        greet([lax.rem(me + i, n_dev) for i in range(1, n_dev)])

    def step(b, carry):
        rows = pl.ds(pl.multiple_of(b * QB, QB), QB)
        keys = pl.ds(pl.multiple_of(b * QB * n_tok, QB * n_tok), n_keys)
        q4 = spread(q_ref[rows, :], mask_b)
        d4 = spread(d_ref[rows, :], mask_b)
        allow = allowed(b, frame, ahead, off_ref[pl.ds(b, 1), :], total)
        scores = jnp.where(allow, dot(k_ref[keys, :], q4, NT) * SCALE, NEG)
        top = jnp.max(scores, axis=0, keepdims=True)
        expo = jnp.exp(scores - top)
        d_probs = dot(v_ref[keys, :], d4, NT)
        owner, row = place(b, per, groups, g)
        mine[owner, 0, row, :] = top
        mine[owner, 1, row, :] = jnp.sum(expo, axis=0, keepdims=True)
        mine[owner, 2, row, :] = jnp.sum(expo * d_probs, axis=0, keepdims=True)
        return carry

    lax.fori_loop(0, total // QB, step, 0, unroll=UNROLL)

    def there(i):
        other = lax.rem(me + i, n_dev)
        return remote(mine.at[other], got.at[i], send.at[i], recv.at[i], other)

    def back(i):
        other = lax.rem(me + i, n_dev)
        return remote(out_ref.at[me], out_ref.at[me], send_back.at[i], recv_back.at[i], other)

    @pl.when(g == groups - 1)
    def _():
        for i in range(1, n_dev):
            there(i).start()
        got[0] = mine[me]
        for i in range(1, n_dev):
            there(i).wait()
        top = got[0, 0]
        for i in range(1, n_dev):
            top = jnp.maximum(top, got[i, 0])
        norm = jnp.zeros_like(top)
        slope = jnp.zeros_like(top)
        for i in range(n_dev):
            factor = jnp.exp(got[i, 0] - top)
            norm = norm + factor * got[i, 1]
            slope = slope + factor * got[i, 2]
        inverse = 1.0 / norm
        out_ref[me, 0] = top
        out_ref[me, 1] = inverse
        out_ref[me, 2] = slope * inverse
        for i in range(1, n_dev):
            back(i).start()
        for i in range(1, n_dev):
            back(i).wait()
        res_ref[...] = out_ref[...]


def value_kernel(
    n_tok, total, n_dev, q_ref, d_ref, k_ref, v_ref, off_ref, st_ref, o_ref, g_ref, acc, ctx
):
    same, mask_b = head_masks()
    frame, ahead = window_parts(n_tok)
    n_keys = frame.shape[0]
    g = pl.program_id(0)
    groups = pl.num_programs(0)
    per = total // QB // n_dev
    acc[...] = jnp.zeros_like(acc)

    def step(b, carry):
        rows = pl.ds(pl.multiple_of(b * QB, QB), QB)
        keys = pl.ds(pl.multiple_of(b * QB * n_tok, QB * n_tok), n_keys)
        q4 = spread(q_ref[rows, :], mask_b)
        d4 = spread(d_ref[rows, :], mask_b)
        allow = allowed(b, frame, ahead, off_ref[pl.ds(b, 1), :], total)
        scores = jnp.where(allow, dot(k_ref[keys, :], q4, NT) * SCALE, NEG)
        owner, row = place(b, per, groups, g)
        probs = jnp.exp(scores - st_ref[owner, 0, row, :]) * st_ref[owner, 1, row, :]
        probs_b = probs.astype(jnp.bfloat16)
        ctx[rows, :] = fold(dot(probs_b, v_ref[keys, :], TN), same)
        acc[keys, :] += dot(probs_b, d4, NN)
        return carry

    lax.fori_loop(0, total // QB, step, 0, unroll=UNROLL)
    o_ref[...] = ctx[...].T.astype(jnp.bfloat16)
    g_ref[...] = acc[...].astype(jnp.bfloat16)


def key_kernel(
    n_tok, total, n_dev, n_bits, q_ref, d_ref, k_ref, v_ref, off_ref, st_ref, a_ref, b_ref,
    dq_ref, g_ref, ao_ref, bo_ref, acc, *rest
):
    same, mask_b = head_masks()
    frame, ahead = window_parts(n_tok)
    n_keys = frame.shape[0]
    g = pl.program_id(0)
    groups = pl.num_programs(0)
    per = total // QB // n_dev
    acc[...] = jnp.zeros_like(acc)
    me = lax.axis_index("tm")
    sums = two_reduces(me, n_bits, (a_ref, b_ref), rest)

    @pl.when(g == 0)
    def _():
        greet([partner_of(me, k) for k in range(n_bits)])
        for one in sums:
            one.copy(0).start()

    def step(b, carry):
        rows = pl.ds(pl.multiple_of(b * QB, QB), QB)
        keys = pl.ds(pl.multiple_of(b * QB * n_tok, QB * n_tok), n_keys)
        q4 = spread(q_ref[rows, :], mask_b)
        d4 = spread(d_ref[rows, :], mask_b)
        allow = allowed(b, frame, ahead, off_ref[pl.ds(b, 1), :], total)
        k_blk = k_ref[keys, :]
        scores = jnp.where(allow, dot(k_blk, q4, NT) * SCALE, NEG)
        owner, row = place(b, per, groups, g)
        probs = jnp.exp(scores - st_ref[owner, 0, row, :]) * st_ref[owner, 1, row, :]
        d_probs = dot(v_ref[keys, :], d4, NT)
        d_scores = probs * (d_probs - st_ref[owner, 2, row, :]) * SCALE
        d_scores = d_scores.astype(jnp.bfloat16)
        dq_ref[rows, :] = fold(dot(d_scores, k_blk, TN), same).astype(jnp.bfloat16)
        acc[keys, :] += dot(d_scores, q4, NN)
        return carry

    lax.fori_loop(0, total // QB, step, 0, unroll=UNROLL)
    g_ref[...] = acc[...].astype(jnp.bfloat16)

    def advance(at):
        for one in sums:
            one.finish(at)
            if at + 1 < n_bits:
                one.copy(at + 1).start()

    n_groups = b_ref.shape[-1] // GW
    for at in range(n_groups):

        @pl.when(g == at)
        def _(at=at):
            last = at + 1 if at + 1 < n_groups else n_bits
            for now in range(at, min(last, n_bits)):
                advance(now)

    @pl.when(g == n_groups - 1)
    def _():
        ao_ref[...] = sums[0].refs[-1][...]
        bo_ref[...] = sums[1].refs[-1][...].astype(jnp.float32)


def two_reduces(me, n_bits, sources, rest):
    send, recv = rest[-2:]
    orders = (low_first(n_bits), late_one(n_bits))
    return [
        Reduce(
            me, n_bits, orders[i], sources[i], rest[i * n_bits : (i + 1) * n_bits],
            send.at[i], recv.at[i],
        )
        for i in range(2)
    ]


def reduce_kernel(n_bits, a_ref, b_ref, ao_ref, bo_ref, *rest):
    me = lax.axis_index("tm")
    sums = two_reduces(me, n_bits, (a_ref, b_ref), rest)
    greet([partner_of(me, k) for k in range(n_bits)])
    for one in sums:
        one.copy(0).start()
    for at in range(n_bits):
        for one in sums:
            one.finish(at)
            if at + 1 < n_bits:
                one.copy(at + 1).start()
    ao_ref[...] = sums[0].refs[-1][...]
    bo_ref[...] = sums[1].refs[-1][...].astype(jnp.float32)


def row_chunk(rows):
    return max(c for c in range(16, 769, 16) if rows % c == 0)


def attention_calls(n_tok, total, width, n_dev):
    n_bits = n_dev.bit_length() - 1
    groups = width // GW
    blocks = total // QB
    here = total // n_dev
    key_rows = (total + 2 * W) * n_tok
    by_query = pl.BlockSpec((total, GW), lambda g: (0, g))
    by_key = pl.BlockSpec((key_rows, GW), lambda g: (0, g))
    by_offset = pl.BlockSpec((blocks, LANES), lambda g: (0, 0))
    by_feature = pl.BlockSpec((GW, total), lambda g: (g, 0))
    whole = pl.BlockSpec(memory_space=pltpu.VMEM)
    key_like = jax.ShapeDtypeStruct((key_rows, width), jnp.bfloat16)
    key_acc = pltpu.VMEM((key_rows, GW), jnp.float32)
    stat = (n_dev, 3, blocks // n_dev * groups, LANES)
    sems = [pltpu.SemaphoreType.DMA((2, n_bits))] * 2
    limit = 56 * 1024 * 1024
    unit = 2 * groups * blocks * (QB + 2 * W) * n_tok * LANES * GW
    common = [by_query, by_query, by_key, by_key, by_offset]
    bits = (2,) * n_bits

    def shape(dims, kind=jnp.bfloat16):
        return jax.ShapeDtypeStruct(dims, kind)

    def params(number):
        return pltpu.CompilerParams(
            vmem_limit_bytes=limit, collective_id=number, has_side_effects=True
        )

    def cost(flops):
        return pl.CostEstimate(
            flops=flops, bytes_accessed=8 * key_rows * width, transcendentals=0
        )

    project = pl.pallas_call(
        functools.partial(project_kernel, n_bits, row_chunk(key_rows)),
        in_specs=[whole] * 5,
        out_specs=[whole] * 4,
        out_shape=[
            shape(bits + (here, width)), shape(bits + (here, width + 128)), key_like, key_like
        ],
        scratch_shapes=sems,
        compiler_params=params(0),
        cost_estimate=cost(4 * key_rows * width * width),
        name="gather_and_project",
    )
    stats = pl.pallas_call(
        functools.partial(stats_kernel, n_tok, total, n_dev),
        grid=(groups,),
        in_specs=common,
        out_specs=whole,
        out_shape=shape(stat, jnp.float32),
        scratch_shapes=[pltpu.VMEM(stat, jnp.float32)] * 3
        + [pltpu.SemaphoreType.DMA((n_dev,))] * 4,
        compiler_params=params(1),
        cost_estimate=cost(8 * unit),
        name="softmax_stats",
    )
    value = pl.pallas_call(
        functools.partial(value_kernel, n_tok, total, n_dev),
        grid=(groups,),
        in_specs=common + [whole],
        out_specs=[by_feature, by_key],
        out_shape=[shape((width, total)), key_like],
        scratch_shapes=[key_acc, pltpu.VMEM((total, GW), jnp.float32)],
        compiler_params=pltpu.CompilerParams(vmem_limit_bytes=limit),
        cost_estimate=cost(12 * unit),
        name="context_and_value_part",
    )
    own = width // n_dev
    key = pl.pallas_call(
        functools.partial(key_kernel, n_tok, total, n_dev, n_bits),
        grid=(groups,),
        in_specs=common + [whole] * 3,
        out_specs=[by_query, by_key, whole, whole],
        out_shape=[
            shape((total, width)), key_like, shape((own, total)), shape((own, width), jnp.float32)
        ],
        scratch_shapes=[key_acc]
        + slot_shapes(n_bits, own, total)
        + slot_shapes(n_bits, own, width)
        + sems,
        compiler_params=params(2),
        cost_estimate=cost(16 * unit),
        name="query_and_key_part",
    )
    reduce = pl.pallas_call(
        functools.partial(reduce_kernel, n_bits),
        in_specs=[whole] * 2,
        out_specs=[whole] * 2,
        out_shape=[shape((here, width)), shape((own, width), jnp.float32)],
        scratch_shapes=slot_shapes(n_bits, here, width) + slot_shapes(n_bits, own, width) + sems,
        compiler_params=params(3),
        cost_estimate=cost(0),
        name="reduce_query_and_key",
    )
    return project, stats, value, key, reduce


def shards(
    exo_tokens, queries, key_weight, value_weight, out_weight, gaze_valid, window_offset, cotangent
):
    rows_here = queries.shape[0]
    width = queries.shape[1]
    total = rows_here * lax.axis_size("tm")
    n_tok = exo_tokens.shape[1]
    blocks = total // QB
    valid_col = gaze_valid.astype(jnp.float32)[:, None]
    masked_grad = (cotangent.astype(jnp.float32) * valid_col).astype(jnp.bfloat16)
    extra = jnp.broadcast_to(window_offset.astype(jnp.bfloat16)[:, None], (rows_here, 128))
    grad_wide = jnp.concatenate([masked_grad, extra], axis=1)
    flat = exo_tokens.reshape(-1, width)
    flat = jnp.pad(flat, ((W * n_tok, W * n_tok), (0, 0)))
    n_dev = lax.axis_size("tm")
    bits = (2,) * (n_dev.bit_length() - 1)
    project, stats, value, key, reduce = attention_calls(n_tok, total, width, n_dev)
    q_all, grad_all, keys, values = project(queries, grad_wide, flat, key_weight, value_weight)
    q_all = q_all.reshape(total, width)
    grad_all = grad_all.reshape(total, -1)
    offsets = grad_all[:, width].astype(jnp.int32).reshape(blocks, 1, QB)
    offsets = jnp.broadcast_to(offsets, (blocks, GH, QB)).reshape(blocks, LANES)
    grad_all = grad_all[:, :width]
    d_context = dot(grad_all, out_weight, NT).astype(jnp.bfloat16)

    common = (q_all, d_context, keys, values, offsets)
    combined = stats(*common)
    context_t, value_part = value(*common, combined)
    value_term = dot(flat, value_part, TN).astype(jnp.bfloat16)
    own = width // n_dev
    d_query, key_part, context_t, d_value = key(
        *common,
        combined,
        context_t.reshape(bits + (own, total)),
        value_term.reshape(bits + (own, width)),
    )
    key_term = dot(flat, key_part, TN).astype(jnp.bfloat16)
    d_query, d_key = reduce(
        d_query.reshape(bits + (rows_here, width)), key_term.reshape(bits + (own, width))
    )
    d_out = dot(context_t, grad_all, NN)
    context = lax.all_to_all(context_t, "tm", split_axis=1, concat_axis=0, tiled=True)
    attended = (dot(context, out_weight, TN) * valid_col).astype(jnp.bfloat16)
    return attended, d_query, d_key, d_value, d_out


def solution(mesh):
    in_specs = (
        P("rep", "tm", None),
        P(("rep", "tm"), None),
        P(),
        P(),
        P(),
        P(("rep", "tm")),
        P(("rep", "tm")),
        P(("rep", "tm"), None),
    )
    out_specs = (P(("rep", "tm"), None),) * 5
    return jax.shard_map(shards, mesh=mesh, in_specs=in_specs, out_specs=out_specs, check_vma=False)
```

time: 597 us -> 266 us (0.45)
  waiting for transfers between devices: 413 us -> 0.01 us
  Pallas kernels: 89.4 us -> 213 us
  matrix products: 44.1 us -> 25.4 us
  between operations: 14.3 us -> 0.78 us
  other arithmetic: 9.96 us -> 2.26 us
    reduce_scatter x4 -> x0, waiting for transfers between devices: 180 us -> none  [the longest x1 62.7 us: shards(): lax.psum_scatter(value_term, 'tm', scatter_dimension=0, tiled=True)]
    pallas_call x3 -> x5, Pallas kernels: 89.4 us -> 213 us  [the longest x1 53.5 us: shards(): key(*common, combined, context_t.reshape(bits + (own, total)), value_term...]
    psum x1 -> x0, waiting for transfers between devices: 90.8 us -> none  [shards(): sums = lax.psum(jnp.stack([norm * factor, slope * factor]), 'tm')]
    pmax x1 -> x0, waiting for transfers between devices: 83.4 us -> none  [shards(): top_all = lax.pmax(top, 'tm')]
    all_gather x2 -> x0, waiting for transfers between devices: 57.6 us -> none  [the longest x1 35.1 us: shards(): q_all = lax.all_gather(queries, 'tm', axis=0, tiled=True)]
    dot_general x7 -> x5, matrix products: 44.1 us -> 25.4 us  [dot(): return lax.dot_general(a, b, dims, preferred_element_type=jnp.float32)]
    unnamed x28 -> x22, local copies, waits for them, and re-layouts: 11.1 us -> 3.34 us
  transfers between devices with their start and end apart: 9 -> 1, of which waited for: 8 -> 0; matrix products, arithmetic and copies ran while one was open for 10% -> 4% of each run, Pallas kernels for 7% -> 17%
where the time goes in v2:
time: 266 us; the launch traced here: 265 us
  Pallas kernels  213 us (80%)
  matrix products  25.4 us (10%)
  local copies, waits for them, and re-layouts  18.6 us (7%)
  starting transfers between devices  4.66 us (2%)
    pallas_call x1, Pallas kernels, shards(): key(*common, combined, context_t.reshape(bits + (own, total)), value_term...  53.5 us
    pallas_call x1, Pallas kernels, shards(): project(queries, grad_wide, flat, key_weight, value_weight)  51.3 us
    pallas_call x1, Pallas kernels, shards(): reduce(d_query.reshape(bits + (rows_here, width)), key_term.reshape(bits...  44.6 us
    pallas_call x1, Pallas kernels, shards(): context_t, value_part = value(*common, combined)  35.4 us
    pallas_call x1, Pallas kernels, shards(): combined = stats(*common)  28.6 us
    dot_general x5, matrix products, dot(): return lax.dot_general(a, b, dims, preferred_element_type=jnp.float32)  25.4 us
    reshape x1, local copies, waits for them, and re-layouts, shards(): flat = exo_tokens.reshape(-1, width)  7.24 us
  transfers between devices with their start and end apart: 1, of which 0 were waited for; matrix products, arithmetic and copies ran while one was open for 4% of the time, Pallas kernels for 17%

profile of v2, /device:TPU:0, one launch (start us, length us, event | category | flops | bytes accessed | tf_op | source)
XLA Modules:
  0.0 265.1 jit_solution(11485395378156235793)
XLA Ops:
  0.6 0.0 copy-start
  0.6 0.8 convert_element_type.37
  1.5 0.7 convert_element_type.39
  2.1 0.0 copy-start.5
  2.1 7.2 %reshape.47 = bf16[2048,1024]{1,0:T(8,128)(2,1)} reshape(bf16[1024,2,1024]{2,1,0:T(2,128)(2,1)} %param.8) | data formatting | bytes 8388608 | tf_op jit(solution)/shard_map/reshape | solution.py:494
  9.4 0.0 copy-done.5
  9.4 0.1 multiply_convert_fusion
  9.4 0.1 broadcast_in_dim.4
  9.5 0.7 pad_maximum_fusion.g_ref
  10.2 4.7 %pad.4.x_ref = bf16[2112,1024]{1,0:T(8,128)(2,1)} pad(bf16[2048,1024]{1,0:T(8,128)(2,1)} %reshape.47, bf16[]{:T(256)} %constant.2.clone.1), padding=32_32x0_0 | pad | bytes 8519682 | tf_op jit(solution)/shard_map/jit(_pad)/pad | solution.py:495
  14.9 51.3 %gather_and_project.1 = (bf16[2,2,2,2,64,1024]{5,4,3,2,1,0:T(8,128)(2,1)}, bf16[2,2,2,2,64,1152]{5,4,3,2,1,0:T(8,128)(2,1)}, bf16[2112,1024]{1,0:T(8,128)(2,1)}, bf16[2112,1024]{1,0:T(8,128)(2,1)}) custom-call(bf16[64,1024]{1,0:T(8,128)(2,1)} %q_ref.1, bf16[64,1152]{1,0:T(8,128)(2,1)} %pad_maximum_fusion.g_ref, bf16[2112,1024]{1,0:T(8,128)(2,1)} %pad.4.x_ref, ...), custom_call_target="tpu_custom_call" | custom-call | flops 8858370048 | bytes 17301504 | tf_op jit(solution)/shard_map/gather_and_project/pallas_call | solution.py:499
  66.2 1.0 slice.9
  67.2 0.1 copy.19
  67.3 0.1 reshape.55
  67.4 0.7 reshape.50.off_ref
  68.1 0.0 copy-done
  68.1 5.3 %convolution_convert_fusion.2.d_ref = bf16[1024,1024]{1,0:T(8,128)(2,1)} fusion(bf16[1024,1024]{1,0:T(8,128)(2,1)S(1)} %copy-done, bf16[1024,1152]{1,0:T(8,128)(2,1)} %bitcast.24), kind=kOutput, calls=%fused_computation.2 | convolution fusion | flops 2148532224 | bytes 6291456 | tf_op jit(solution)/shard_map/dot_general | solution.py:27
  73.5 28.6 %softmax_stats.1.st_ref = f32[16,3,8,128]{3,2,1,0:T(8,128)} custom-call(bf16[1024,1024]{1,0:T(8,128)(2,1)} %bitcast.26, bf16[1024,1024]{1,0:T(8,128)(2,1)} %convolution_convert_fusion.2.d_ref, bf16[2112,1024]{1,0:T(8,128)(2,1)} %get-tuple-element.19.k_ref, bf16[2112,1024]{1,0:T(8,128)(2,1)} %get-tuple-element.20.v_ref, s32[32,128]{1,0:T(8,128)} %reshape.50.off_ref), custom_call_target="tpu_custom_call" | custom-call | flops 8589934592 | bytes 17301504 | tf_op jit(solution)/shard_map/softmax_stats/pallas_call | solution.py:508
  102.1 0.0 copy-start.1
  102.1 35.4 %context_and_value_part.1 = (bf16[1024,1024]{1,0:T(8,128)(2,1)}, bf16[2112,1024]{1,0:T(8,128)(2,1)}) custom-call(bf16[1024,1024]{1,0:T(8,128)(2,1)} %bitcast.27, bf16[1024,1024]{1,0:T(8,128)(2,1)} %convolution_convert_fusion.2.d_ref, bf16[2112,1024]{1,0:T(8,128)(2,1)} %get-tuple-element.19.k_ref, bf16[2112,1024]{1,0:T(8,128)(2,1)} %get-tuple-element.20.v_ref, ...), custom_call_target="tpu_custom_call" | custom-call | flops 12884901888 | bytes 17301504 | tf_op jit(solution)/shard_map/context_and_value_part/pallas_call | solution.py:509
  137.5 0.0 copy-done.1
  137.5 8.6 %convolution_convert_fusion.1 = bf16[1024,1024]{1,0:T(8,128)(2,1)} fusion(bf16[2112,1024]{1,0:T(8,128)(2,1)} %get-tuple-element.22, bf16[2048,1024]{1,0:T(8,128)(2,1)S(1)} %copy-done.1), kind=kOutput, calls=%fused_computation.1 | convolution fusion | flops 4430233600 | bytes 10616832 | tf_op jit(solution)/shard_map/dot_general | solution.py:27
  146.2 53.5 %query_and_key_part.1 = (bf16[1024,1024]{1,0:T(8,128)(2,1)}, bf16[2112,1024]{1,0:T(8,128)(2,1)}, bf16[64,1024]{1,0:T(8,128)(2,1)}, f32[64,1024]{1,0:T(8,128)}) custom-call(bf16[1024,1024]{1,0:T(8,128)(2,1)} %bitcast.28, bf16[1024,1024]{1,0:T(8,128)(2,1)} %convolution_convert_fusion.2.d_ref, bf16[2112,1024]{1,0:T(8,128)(2,1)} %get-tuple-element.19.k_ref, ...), custom_call_target="tpu_custom_call" | custom-call | flops 17179869184 | bytes 17301504 | tf_op jit(solution)/shard_map/query_and_key_part/pallas_call | solution.py:512
  199.6 1.1 copy.18
  200.7 0.9 reshape.63
  201.6 4.7 %all-to-all-start = ((bf16[16,2,2048]{2,1,0:T(2,128)(2,1)}), bf16[16,2,2048]{2,1,0:T(2,128)(2,1)S(1)}, u32[]{:S(2)}, u32[]{:S(2)}) async-start(bf16[16,2,2048]{2,1,0:T(2,128)(2,1)} %reshape.63), calls=%async_computation | async-start | bytes 262144 | tf_op jit(solution)/shard_map/all_to_all | solution.py:523
  206.3 9.1 %convolution_convert_fusion = bf16[1024,1024]{1,0:T(8,128)(2,1)} fusion(bf16[2112,1024]{1,0:T(8,128)(2,1)} %get-tuple-element.25, bf16[2048,1024]{1,0:T(8,128)(2,1)} %reshape.47), kind=kOutput, calls=%fused_computation | convolution fusion | flops 4430233600 | bytes 10616832 | tf_op jit(solution)/shard_map/dot_general | solution.py:27
  215.4 0.0 copy-start.4
  215.4 0.0 copy-start.7
  215.4 44.6 %reduce_query_and_key.1 = (bf16[64,1024]{1,0:T(8,128)(2,1)}, f32[64,1024]{1,0:T(8,128)}) custom-call(bf16[2,2,2,2,64,1024]{5,4,3,2,1,0:T(8,128)(2,1)} %bitcast.20, bf16[2,2,2,2,64,1024]{5,4,3,2,1,0:T(8,128)(2,1)} %bitcast.21), custom_call_target="tpu_custom_call" | custom-call | bytes 17301504 | tf_op jit(solution)/shard_map/reduce_query_and_key/pallas_call | solution.py:519
  260.1 0.0 copy-done.4
  260.1 0.0 copy-done.7
  260.1 1.2 fusion
  261.3 0.0 copy-start.6
  261.3 0.0 copy-start.3
  261.3 0.0 all-to-all-done
  261.3 0.2 reshape.64
  261.5 0.0 copy-start.2
  261.5 0.2 copy.17
  261.7 0.2 all_to_all.17
  261.9 1.1 fusion.3
  263.1 0.0 copy-done.6
  263.1 0.7 copy.23
  263.7 0.0 copy-done.3
  263.7 0.7 copy.24
  264.4 0.0 copy-done.2
  264.4 0.7 copy.25
  (3 shorter events, 0.1 us)
Async XLA Ops:
  0.6 67.5 %copy-start = (bf16[1024,1024]{1,0:T(8,128)(2,1)S(1)}, bf16[1024,1024]{1,0:T(8,128)(2,1)}, u32[]{:S(2)}) copy-start(bf16[1024,1024]{1,0:T(8,128)(2,1)} %param.12) | copy-start | bytes 6291460
  2.1 7.2 %copy-start.5 = (bf16[64,1024]{1,0:T(8,128)(2,1)S(1)}, bf16[64,1024]{1,0:T(8,128)(2,1)}, u32[]{:S(2)}) copy-start(bf16[64,1024]{1,0:T(8,128)(2,1)} %param.15) | copy-start | bytes 393220
  102.1 35.4 %copy-start.1 = (bf16[2048,1024]{1,0:T(8,128)(2,1)S(1)}, bf16[2048,1024]{1,0:T(8,128)(2,1)}, u32[]{:S(2)}) copy-start(bf16[2048,1024]{1,0:T(8,128)(2,1)} %reshape.47) | copy-start | bytes 12582916
  201.6 59.6 %all-to-all-start = ((bf16[16,2,2048]{2,1,0:T(2,128)(2,1)}), bf16[16,2,2048]{2,1,0:T(2,128)(2,1)S(1)}, u32[]{:S(2)}, u32[]{:S(2)}) async-start(bf16[16,2,2048]{2,1,0:T(2,128)(2,1)} %reshape.63), calls=%async_computation | async-start | bytes 262144 | tf_op jit(solution)/shard_map/all_to_all | solution.py:523
  215.4 44.7 %copy-start.4 = (bf16[64,1024]{1,0:T(8,128)(2,1)S(1)}, bf16[64,1024]{1,0:T(8,128)(2,1)}, u32[]{:S(2)}) copy-start(bf16[64,1024]{1,0:T(8,128)(2,1)} %get-tuple-element.23) | copy-start | bytes 393220
  215.4 44.7 %copy-start.7 = (bf16[2,2,2,2,64,1152]{5,4,3,2,1,0:T(8,128)(2,1)S(1)}, bf16[2,2,2,2,64,1152]{5,4,3,2,1,0:T(8,128)(2,1)}, u32[]{:S(2)}) copy-start(bf16[2,2,2,2,64,1152]{5,4,3,2,1,0:T(8,128)(2,1)} %get-tuple-element.18) | copy-start | bytes 7077892
  261.3 1.8 copy-start.6
  261.3 2.4 copy-start.3
  261.5 2.9 %copy-start.2 = (f32[64,1024]{1,0:T(8,128)S(1)}, f32[64,1024]{1,0:T(8,128)}, u32[]{:S(2)}) copy-start(f32[64,1024]{1,0:T(8,128)} %get-tuple-element.37) | copy-start | bytes 786436

commit v3 on v2

--- a/solution.py
+++ b/solution.py
@@ -31,19 +31,21 @@
     return jnp.concatenate([rows] * GH, axis=0) * head_mask
 
 
-def fold(wide, head_mask):
-    kept = jnp.where(head_mask, wide, 0.0)
-    total = kept[0:QB]
-    for h in range(1, GH):
-        total = total + kept[h * QB : (h + 1) * QB]
-    return total
-
-
-def head_masks():
+def fold(wide):
+    lane = lax.broadcasted_iota(jnp.int32, (QB, 2 * HD), 1)
+    tiles = []
+    for h in range(0, GH, 2):
+        cols = slice(h * HD, (h + 2) * HD)
+        first = wide[h * QB : (h + 1) * QB, cols]
+        second = wide[(h + 1) * QB : (h + 2) * QB, cols]
+        tiles.append(jnp.where(lane < HD, first, second))
+    return jnp.concatenate(tiles, axis=1)
+
+
+def head_mask():
     row = lax.broadcasted_iota(jnp.int32, (LANES, GW), 0) // QB
     col = lax.broadcasted_iota(jnp.int32, (LANES, GW), 1) // HD
-    same = row == col
-    return same, jnp.where(same, 1.0, 0.0).astype(jnp.bfloat16)
+    return jnp.where(row == col, 1.0, 0.0).astype(jnp.bfloat16)
 
 
 def window_parts(n_tok):
@@ -106,10 +108,11 @@
 
 
 class Reduce:
-    def __init__(self, me, n_bits, order, src, slots, send, recv):
-        self.me, self.order = me, order
+    def __init__(self, me, n_bits, src, first_col, slots, send, recv):
+        self.me, self.order = me, list(range(n_bits))
         self.bits = list(range(n_bits))[::-1]
-        self.refs = [src] + list(slots)
+        self.src, self.slots = src, slots
+        self.cols = pl.ds(first_col, slots[0].shape[-1])
         self.send, self.recv = send, recv
 
     def left(self, step):
@@ -117,9 +120,15 @@
 
     def copy(self, step):
         k = self.order[step]
-        part = at_bits(self.refs[step], self.left(step), {k: 1 - bit_of(self.me, k)})
+        index = tuple(
+            1 - bit_of(self.me, k) if bit == k else slice(None) for bit in self.left(step)
+        )
+        if step == 0:
+            part = self.src.at[index + (slice(None), self.cols)]
+        else:
+            part = self.slots[step - 1].at[index]
         other = partner_of(self.me, k)
-        return remote(part, self.refs[step + 1], self.send.at[step], self.recv.at[step], other)
+        return remote(part, self.slots[step], self.send.at[step], self.recv.at[step], other)
 
     def finish(self, step):
         self.copy(step).wait()
@@ -129,10 +138,40 @@
         for index in itertools.product((0, 1), repeat=len(rest)):
             chosen = dict(zip(rest, index))
             chosen[k] = bit_of(self.me, k)
-            own = self.refs[step][tuple(chosen[bit] for bit in bits)]
-            got = self.refs[step + 1][index]
-            total = own.astype(jnp.float32) + got.astype(jnp.float32)
-            self.refs[step + 1][index] = total.astype(jnp.bfloat16)
+            at = tuple(chosen[bit] for bit in bits)
+            if step == 0:
+                own = self.src[at + (slice(None), self.cols)]
+            else:
+                own = self.slots[step - 1][at]
+            total = own.astype(jnp.float32) + self.slots[step][index].astype(jnp.float32)
+            self.slots[step][index] = total.astype(jnp.bfloat16)
+
+
+class Staged:
+    def __init__(self, sums, starts, n_bits):
+        self.sums, self.starts, self.n_bits = sums, starts, n_bits
+        self.ticks = max(starts) + n_bits
+
+    def begin(self, at):
+        for one, start in zip(self.sums, self.starts):
+            if start == at:
+                one.copy(0).start()
+
+    def tick(self, at):
+        for one, start in zip(self.sums, self.starts):
+            step = at - start
+            if 0 <= step < self.n_bits:
+                one.finish(step)
+                if step + 1 < self.n_bits:
+                    one.copy(step + 1).start()
+        self.begin(at + 1)
+
+    def write(self, refs):
+        half = len(self.sums) // 2
+        for i, ref in enumerate(refs):
+            for j in range(half):
+                one = self.sums[i * half + j]
+                ref[:, one.cols] = one.slots[-1][...].astype(ref.dtype)
 
 
 def slot_shapes(n_bits, rows, width):
@@ -142,47 +181,47 @@
     ]
 
 
-def low_first(n_bits):
-    return list(range(n_bits))
-
-
-def late_one(n_bits):
-    return [0] + list(range(2, n_bits)) + [1]
-
-
 def project_kernel(
     n_bits, chunk, q_ref, g_ref, x_ref, kw_ref, vw_ref, qo_ref, go_ref, k_ref, v_ref, send, recv
 ):
     me = lax.axis_index("tm")
     greet([partner_of(me, k) for k in range(n_bits)])
-    orders = (list(range(1, n_bits))[::-1] + [0], [1] + list(range(2, n_bits))[::-1] + [0])
+    order = list(range(n_bits))[::-1]
     gathers = []
     for i, (mine, out) in enumerate(((q_ref, qo_ref), (g_ref, go_ref))):
         out[tuple(bit_of(me, k) for k in range(n_bits)[::-1])] = mine[...]
-        gathers.append(Gather(me, n_bits, orders[i], out, send.at[i], recv.at[i]))
-    for gather in gathers:
-        gather.copy(0).start()
+        gathers.append(Gather(me, n_bits, order, out, send.at[i], recv.at[i]))
+    gathers[0].copy(0).start()
     rows, width = x_ref.shape
     n_cols = width // GW
+    pad = (k_ref.shape[0] - rows) // 2
+    for ref in (k_ref, v_ref):
+        ref[:pad, :] = jnp.zeros((pad, width), jnp.bfloat16)
+        ref[rows + pad :, :] = jnp.zeros((pad, width), jnp.bfloat16)
 
     def piece(j, carry):
         cols = pl.ds(pl.multiple_of(j * GW, GW), GW)
 
         def part(i, inner):
             here = pl.ds(pl.multiple_of(i * chunk, 16), chunk)
+            there = pl.ds(pl.multiple_of(i * chunk + pad, 16), chunk)
             x = x_ref[here, :]
-            k_ref[here, cols] = dot(x, kw_ref[:, cols], NN).astype(jnp.bfloat16)
-            v_ref[here, cols] = dot(x, vw_ref[:, cols], NN).astype(jnp.bfloat16)
+            k_ref[there, cols] = dot(x, kw_ref[:, cols], NN).astype(jnp.bfloat16)
+            v_ref[there, cols] = dot(x, vw_ref[:, cols], NN).astype(jnp.bfloat16)
             return inner
 
         lax.fori_loop(0, rows // chunk, part, 0)
         return carry
 
-    for step in range(n_bits):
-        lax.fori_loop(n_cols * step // n_bits, n_cols * (step + 1) // n_bits, piece, 0)
-        for gather in gathers:
-            gather.copy(step).wait()
-            if step + 1 < n_bits:
+    lag = 2
+    ticks = n_bits + lag
+    for tick in range(ticks):
+        lax.fori_loop(n_cols * tick // ticks, n_cols * (tick + 1) // ticks, piece, 0)
+        for gather, start in zip(gathers, (0, lag)):
+            step = tick - start
+            if 0 <= step < n_bits:
+                gather.copy(step).wait()
+            if 0 <= step + 1 < n_bits:
                 gather.copy(step + 1).start()
 
 
@@ -194,7 +233,7 @@
     n_tok, total, n_dev, q_ref, d_ref, k_ref, v_ref, off_ref, res_ref, mine, got, out_ref,
     send, recv, send_back, recv_back,
 ):
-    _, mask_b = head_masks()
+    mask_b = head_mask()
     frame, ahead = window_parts(n_tok)
     n_keys = frame.shape[0]
     g = pl.program_id(0)
@@ -262,17 +301,19 @@
 def value_kernel(
     n_tok, total, n_dev, q_ref, d_ref, k_ref, v_ref, off_ref, st_ref, o_ref, g_ref, acc, ctx
 ):
-    same, mask_b = head_masks()
+    mask_b = head_mask()
     frame, ahead = window_parts(n_tok)
     n_keys = frame.shape[0]
+    ahead_rows = QB * n_tok
+    pad = W * n_tok
     g = pl.program_id(0)
     groups = pl.num_programs(0)
     per = total // QB // n_dev
-    acc[...] = jnp.zeros_like(acc)
 
     def step(b, carry):
         rows = pl.ds(pl.multiple_of(b * QB, QB), QB)
-        keys = pl.ds(pl.multiple_of(b * QB * n_tok, QB * n_tok), n_keys)
+        first = pl.multiple_of(b * ahead_rows, ahead_rows)
+        keys = pl.ds(first, n_keys)
         q4 = spread(q_ref[rows, :], mask_b)
         d4 = spread(d_ref[rows, :], mask_b)
         allow = allowed(b, frame, ahead, off_ref[pl.ds(b, 1), :], total)
@@ -280,38 +321,42 @@
         owner, row = place(b, per, groups, g)
         probs = jnp.exp(scores - st_ref[owner, 0, row, :]) * st_ref[owner, 1, row, :]
         probs_b = probs.astype(jnp.bfloat16)
-        ctx[rows, :] = fold(dot(probs_b, v_ref[keys, :], TN), same)
-        acc[keys, :] += dot(probs_b, d4, NN)
-        return carry
-
-    lax.fori_loop(0, total // QB, step, 0, unroll=UNROLL)
+        ctx[rows, :] = fold(dot(probs_b, v_ref[keys, :], TN))
+        part = dot(probs_b, d4, NN)
+        acc[pl.ds(first, ahead_rows), :] = (carry + part[:ahead_rows]).astype(jnp.bfloat16)
+        return part[ahead_rows:]
+
+    zero = jnp.zeros((ahead_rows, GW), jnp.float32)
+    tail = lax.fori_loop(0, total // QB, step, zero, unroll=UNROLL)
+    acc[total * n_tok :, :] = tail.astype(jnp.bfloat16)
     o_ref[...] = ctx[...].T.astype(jnp.bfloat16)
-    g_ref[...] = acc[...].astype(jnp.bfloat16)
+    g_ref[...] = acc[pad : pad + total * n_tok, :]
 
 
 def key_kernel(
     n_tok, total, n_dev, n_bits, q_ref, d_ref, k_ref, v_ref, off_ref, st_ref, a_ref, b_ref,
     dq_ref, g_ref, ao_ref, bo_ref, acc, *rest
 ):
-    same, mask_b = head_masks()
+    mask_b = head_mask()
     frame, ahead = window_parts(n_tok)
     n_keys = frame.shape[0]
+    ahead_rows = QB * n_tok
+    pad = W * n_tok
     g = pl.program_id(0)
     groups = pl.num_programs(0)
     per = total // QB // n_dev
-    acc[...] = jnp.zeros_like(acc)
     me = lax.axis_index("tm")
-    sums = two_reduces(me, n_bits, (a_ref, b_ref), rest)
+    staged = Staged(four_sums(me, n_bits, (a_ref, b_ref), rest), (0, 1, 2, 3), n_bits)
 
     @pl.when(g == 0)
     def _():
         greet([partner_of(me, k) for k in range(n_bits)])
-        for one in sums:
-            one.copy(0).start()
+        staged.begin(0)
 
     def step(b, carry):
         rows = pl.ds(pl.multiple_of(b * QB, QB), QB)
-        keys = pl.ds(pl.multiple_of(b * QB * n_tok, QB * n_tok), n_keys)
+        first = pl.multiple_of(b * ahead_rows, ahead_rows)
+        keys = pl.ds(first, n_keys)
         q4 = spread(q_ref[rows, :], mask_b)
         d4 = spread(d_ref[rows, :], mask_b)
         allow = allowed(b, frame, ahead, off_ref[pl.ds(b, 1), :], total)
@@ -322,59 +367,64 @@
         d_probs = dot(v_ref[keys, :], d4, NT)
         d_scores = probs * (d_probs - st_ref[owner, 2, row, :]) * SCALE
         d_scores = d_scores.astype(jnp.bfloat16)
-        dq_ref[rows, :] = fold(dot(d_scores, k_blk, TN), same).astype(jnp.bfloat16)
-        acc[keys, :] += dot(d_scores, q4, NN)
-        return carry
-
-    lax.fori_loop(0, total // QB, step, 0, unroll=UNROLL)
-    g_ref[...] = acc[...].astype(jnp.bfloat16)
-
-    def advance(at):
-        for one in sums:
-            one.finish(at)
-            if at + 1 < n_bits:
-                one.copy(at + 1).start()
+        dq_ref[rows, :] = fold(dot(d_scores, k_blk, TN)).astype(jnp.bfloat16)
+        part = dot(d_scores, q4, NN)
+        acc[pl.ds(first, ahead_rows), :] = (carry + part[:ahead_rows]).astype(jnp.bfloat16)
+        return part[ahead_rows:]
 
     n_groups = b_ref.shape[-1] // GW
-    for at in range(n_groups):
-
-        @pl.when(g == at)
-        def _(at=at):
-            last = at + 1 if at + 1 < n_groups else n_bits
-            for now in range(at, min(last, n_bits)):
-                advance(now)
+    points = 2 * n_groups
+    half = total // QB // 2
+    tail = jnp.zeros((ahead_rows, GW), jnp.float32)
+    for side in range(2):
+        tail = lax.fori_loop(side * half, (side + 1) * half, step, tail, unroll=UNROLL)
+        for at in range(side, points, 2):
+
+            @pl.when(g == at // 2)
+            def _(at=at):
+                last = at + 1 if at + 1 < points else staged.ticks
+                for now in range(at, min(last, staged.ticks)):
+                    staged.tick(now)
+
+    acc[total * n_tok :, :] = tail.astype(jnp.bfloat16)
+    g_ref[...] = acc[pad : pad + total * n_tok, :]
 
     @pl.when(g == n_groups - 1)
     def _():
-        ao_ref[...] = sums[0].refs[-1][...]
-        bo_ref[...] = sums[1].refs[-1][...].astype(jnp.float32)
-
-
-def two_reduces(me, n_bits, sources, rest):
+        staged.write((ao_ref, bo_ref))
+
+
+def four_sums(me, n_bits, sources, rest):
     send, recv = rest[-2:]
-    orders = (low_first(n_bits), late_one(n_bits))
-    return [
-        Reduce(
-            me, n_bits, orders[i], sources[i], rest[i * n_bits : (i + 1) * n_bits],
-            send.at[i], recv.at[i],
-        )
-        for i in range(2)
-    ]
-
-
-def reduce_kernel(n_bits, a_ref, b_ref, ao_ref, bo_ref, *rest):
+    sums = []
+    for i in range(4):
+        slots = rest[i * n_bits : (i + 1) * n_bits]
+        first_col = (i % 2) * slots[0].shape[-1]
+        source = sources[i // 2]
+        sums.append(Reduce(me, n_bits, source, first_col, slots, send.at[i], recv.at[i]))
+    return sums
+
+
+def reduce_kernel(n_bits, a_ref, x_ref, g_ref, ao_ref, bo_ref, term, *rest):
     me = lax.axis_index("tm")
-    sums = two_reduces(me, n_bits, (a_ref, b_ref), rest)
+    staged = Staged(four_sums(me, n_bits, (a_ref, term), rest), (0, 1, 2, 4), n_bits)
     greet([partner_of(me, k) for k in range(n_bits)])
-    for one in sums:
-        one.copy(0).start()
-    for at in range(n_bits):
-        for one in sums:
-            one.finish(at)
-            if at + 1 < n_bits:
-                one.copy(at + 1).start()
-    ao_ref[...] = sums[0].refs[-1][...]
-    bo_ref[...] = sums[1].refs[-1][...].astype(jnp.float32)
+    staged.begin(0)
+    width = x_ref.shape[1]
+    own = term.shape[-2]
+    half = width // 2
+    for tick in range(staged.ticks):
+        if tick < 4:
+            cols = slice(tick // 2 * half, (tick // 2 + 1) * half)
+            for first in range(tick % 2 * half, (tick % 2 + 1) * half, GW):
+                product = dot(x_ref[:, first : first + GW], g_ref[:, cols], TN)
+                product = product.astype(jnp.bfloat16)
+                for i in range(GW // own):
+                    owner = first // own + i
+                    index = tuple((owner >> k) % 2 for k in range(n_bits)[::-1])
+                    term[index + (slice(None), cols)] = product[i * own : (i + 1) * own]
+        staged.tick(tick)
+    staged.write((ao_ref, bo_ref))
 
 
 def row_chunk(rows):
@@ -393,9 +443,11 @@
     by_feature = pl.BlockSpec((GW, total), lambda g: (g, 0))
     whole = pl.BlockSpec(memory_space=pltpu.VMEM)
     key_like = jax.ShapeDtypeStruct((key_rows, width), jnp.bfloat16)
-    key_acc = pltpu.VMEM((key_rows, GW), jnp.float32)
+    part_like = jax.ShapeDtypeStruct((total * n_tok, width), jnp.bfloat16)
+    by_part = pl.BlockSpec((total * n_tok, GW), lambda g: (0, g))
+    key_acc = pltpu.VMEM((key_rows, GW), jnp.bfloat16)
     stat = (n_dev, 3, blocks // n_dev * groups, LANES)
-    sems = [pltpu.SemaphoreType.DMA((2, n_bits))] * 2
+    sems = [pltpu.SemaphoreType.DMA((4, n_bits))] * 2
     limit = 56 * 1024 * 1024
     unit = 2 * groups * blocks * (QB + 2 * W) * n_tok * LANES * GW
     common = [by_query, by_query, by_key, by_key, by_offset]
@@ -415,7 +467,7 @@
         )
 
     project = pl.pallas_call(
-        functools.partial(project_kernel, n_bits, row_chunk(key_rows)),
+        functools.partial(project_kernel, n_bits, row_chunk(total * n_tok)),
         in_specs=[whole] * 5,
         out_specs=[whole] * 4,
         out_shape=[
@@ -442,8 +494,8 @@
         functools.partial(value_kernel, n_tok, total, n_dev),
         grid=(groups,),
         in_specs=common + [whole],
-        out_specs=[by_feature, by_key],
-        out_shape=[shape((width, total)), key_like],
+        out_specs=[by_feature, by_part],
+        out_shape=[shape((width, total)), part_like],
         scratch_shapes=[key_acc, pltpu.VMEM((total, GW), jnp.float32)],
         compiler_params=pltpu.CompilerParams(vmem_limit_bytes=limit),
         cost_estimate=cost(12 * unit),
@@ -454,13 +506,13 @@
         functools.partial(key_kernel, n_tok, total, n_dev, n_bits),
         grid=(groups,),
         in_specs=common + [whole] * 3,
-        out_specs=[by_query, by_key, whole, whole],
+        out_specs=[by_query, by_part, whole, whole],
         out_shape=[
-            shape((total, width)), key_like, shape((own, total)), shape((own, width), jnp.float32)
+            shape((total, width)), part_like, shape((own, total)), shape((own, width), jnp.float32)
         ],
         scratch_shapes=[key_acc]
-        + slot_shapes(n_bits, own, total)
-        + slot_shapes(n_bits, own, width)
+        + slot_shapes(n_bits, own, total // 2) * 2
+        + slot_shapes(n_bits, own, width // 2) * 2
         + sems,
         compiler_params=params(2),
         cost_estimate=cost(16 * unit),
@@ -468,12 +520,15 @@
     )
     reduce = pl.pallas_call(
         functools.partial(reduce_kernel, n_bits),
-        in_specs=[whole] * 2,
+        in_specs=[whole] * 3,
         out_specs=[whole] * 2,
         out_shape=[shape((here, width)), shape((own, width), jnp.float32)],
-        scratch_shapes=slot_shapes(n_bits, here, width) + slot_shapes(n_bits, own, width) + sems,
+        scratch_shapes=[pltpu.VMEM(bits + (own, width), jnp.bfloat16)]
+        + slot_shapes(n_bits, here, width // 2) * 2
+        + slot_shapes(n_bits, own, width // 2) * 2
+        + sems,
         compiler_params=params(3),
-        cost_estimate=cost(0),
+        cost_estimate=cost(2 * key_rows * width * width),
         name="reduce_query_and_key",
     )
     return project, stats, value, key, reduce
@@ -492,7 +547,6 @@
     extra = jnp.broadcast_to(window_offset.astype(jnp.bfloat16)[:, None], (rows_here, 128))
     grad_wide = jnp.concatenate([masked_grad, extra], axis=1)
     flat = exo_tokens.reshape(-1, width)
-    flat = jnp.pad(flat, ((W * n_tok, W * n_tok), (0, 0)))
     n_dev = lax.axis_size("tm")
     bits = (2,) * (n_dev.bit_length() - 1)
     project, stats, value, key, reduce = attention_calls(n_tok, total, width, n_dev)
@@ -515,10 +569,7 @@
         context_t.reshape(bits + (own, total)),
         value_term.reshape(bits + (own, width)),
     )
-    key_term = dot(flat, key_part, TN).astype(jnp.bfloat16)
-    d_query, d_key = reduce(
-        d_query.reshape(bits + (rows_here, width)), key_term.reshape(bits + (own, width))
-    )
+    d_query, d_key = reduce(d_query.reshape(bits + (rows_here, width)), flat, key_part)
     d_out = dot(context_t, grad_all, NN)
     context = lax.all_to_all(context_t, "tm", split_axis=1, concat_axis=0, tiled=True)
     attended = (dot(context, out_weight, TN) * valid_col).astype(jnp.bfloat16)

time: 266 us -> 259 us (0.974)
  matrix products: 25.4 us -> 15.7 us
  Pallas kernels: 213 us -> 222 us
  local copies, waits for them, and re-layouts: 18.6 us -> 13.9 us
    dot_general x5 -> x4, matrix products: 25.4 us -> 15.7 us  [dot(): return lax.dot_general(a, b, dims, preferred_element_type=jnp.float32)]
    pallas_call x1, Pallas kernels: 51.3 us -> 60.1 us  [shards(): project(queries, grad_wide, flat, key_weight, value_weight)]
    pallas_call x1, Pallas kernels: 35.4 us -> 27.2 us  [shards(): context_t, value_part = value(*common, combined)]
    pallas_call x1, Pallas kernels: 44.6 us -> 49.9 us  [shards(): reduce(d_query.reshape(bits + (rows_here, width)), flat, key_part)]
    pad x1 -> x0, local copies, waits for them, and re-layouts: 4.69 us -> none  [shards(): flat = jnp.pad(flat, ((W * n_tok, W * n_tok), (0, 0)))]
    pallas_call x1, Pallas kernels: 28.6 us -> 31.7 us  [shards(): combined = stats(*common)]
  transfers between devices with their start and end apart: 1 -> 1, of which waited for: 0 -> 0; matrix products, arithmetic and copies ran while one was open for 4% -> 0% of each run, Pallas kernels for 17% -> 19%
where the time goes in v3:
time: 259 us; the launch traced here: 258 us
  Pallas kernels  222 us (86%)
  matrix products  15.7 us (6%)
  local copies, waits for them, and re-layouts  13.9 us (5%)
  starting transfers between devices  3.69 us (1%)
    pallas_call x1, Pallas kernels, shards(): project(queries, grad_wide, flat, key_weight, value_weight)  60.1 us
    pallas_call x1, Pallas kernels, shards(): key(*common, combined, context_t.reshape(bits + (own, total)), value_term...  53.1 us
    pallas_call x1, Pallas kernels, shards(): reduce(d_query.reshape(bits + (rows_here, width)), flat, key_part)  49.9 us
    pallas_call x1, Pallas kernels, shards(): combined = stats(*common)  31.7 us
    pallas_call x1, Pallas kernels, shards(): context_t, value_part = value(*common, combined)  27.2 us
    dot_general x4, matrix products, dot(): return lax.dot_general(a, b, dims, preferred_element_type=jnp.float32)  15.7 us
    reshape x1, local copies, waits for them, and re-layouts, shards(): flat = exo_tokens.reshape(-1, width)  7.26 us
  transfers between devices with their start and end apart: 1, of which 0 were waited for; matrix products, arithmetic and copies ran while one was open for 0% of the time, Pallas kernels for 19%

profile of v3, /device:TPU:0, one launch (start us, length us, event | category | flops | bytes accessed | tf_op | source)
XLA Modules:
  0.0 258.5 jit_solution(15629181011129397423)
XLA Ops:
  0.6 0.0 copy-start
  0.6 0.8 convert_element_type.35
  1.5 0.7 convert_element_type.37
  2.1 0.0 copy-start.5
  2.1 7.3 %reshape.44.x_ref = bf16[2048,1024]{1,0:T(8,128)(2,1)} reshape(bf16[1024,2,1024]{2,1,0:T(2,128)(2,1)} %param.8) | data formatting | bytes 8388608 | tf_op jit(solution)/shard_map/reshape | solution.py:549
  9.4 0.0 copy-done.5
  9.4 0.1 multiply_convert_fusion
  9.5 0.1 broadcast_in_dim.4
  9.5 0.7 pad_maximum_fusion.g_ref
  10.2 60.1 %gather_and_project.1 = (bf16[2,2,2,2,64,1024]{5,4,3,2,1,0:T(8,128)(2,1)}, bf16[2,2,2,2,64,1152]{5,4,3,2,1,0:T(8,128)(2,1)}, bf16[2112,1024]{1,0:T(8,128)(2,1)}, bf16[2112,1024]{1,0:T(8,128)(2,1)}) custom-call(bf16[64,1024]{1,0:T(8,128)(2,1)} %q_ref.1, bf16[64,1152]{1,0:T(8,128)(2,1)} %pad_maximum_fusion.g_ref, bf16[2048,1024]{1,0:T(8,128)(2,1)} %reshape.44.x_ref, ...), custom_call_target="tpu_custom_call" | custom-call | flops 8858370048 | bytes 17301504 | tf_op jit(solution)/shard_map/gather_and_project/pallas_call | solution.py:553
  70.3 1.0 slice.9
  71.3 0.1 copy.19
  71.5 0.1 reshape.51
  71.6 0.7 reshape.47.off_ref
  72.3 0.0 copy-done
  72.3 5.4 %convolution_convert_fusion.1.d_ref = bf16[1024,1024]{1,0:T(8,128)(2,1)} fusion(bf16[1024,1024]{1,0:T(8,128)(2,1)S(1)} %copy-done, bf16[1024,1152]{1,0:T(8,128)(2,1)} %bitcast.23), kind=kOutput, calls=%fused_computation.1 | convolution fusion | flops 2148532224 | bytes 6291456 | tf_op jit(solution)/shard_map/dot_general | solution.py:27
  77.6 31.7 %softmax_stats.1.st_ref = f32[16,3,8,128]{3,2,1,0:T(8,128)} custom-call(bf16[1024,1024]{1,0:T(8,128)(2,1)} %bitcast.25, bf16[1024,1024]{1,0:T(8,128)(2,1)} %convolution_convert_fusion.1.d_ref, bf16[2112,1024]{1,0:T(8,128)(2,1)} %get-tuple-element.19.k_ref, bf16[2112,1024]{1,0:T(8,128)(2,1)} %get-tuple-element.20.v_ref, s32[32,128]{1,0:T(8,128)} %reshape.47.off_ref), custom_call_target="tpu_custom_call" | custom-call | flops 8589934592 | bytes 17301504 | tf_op jit(solution)/shard_map/softmax_stats/pallas_call | solution.py:562
  109.4 0.0 copy-start.1
  109.4 27.2 %context_and_value_part.1 = (bf16[1024,1024]{1,0:T(8,128)(2,1)}, bf16[2048,1024]{1,0:T(8,128)(2,1)}) custom-call(bf16[1024,1024]{1,0:T(8,128)(2,1)} %bitcast.26, bf16[1024,1024]{1,0:T(8,128)(2,1)} %convolution_convert_fusion.1.d_ref, bf16[2112,1024]{1,0:T(8,128)(2,1)} %get-tuple-element.19.k_ref, bf16[2112,1024]{1,0:T(8,128)(2,1)} %get-tuple-element.20.v_ref, ...), custom_call_target="tpu_custom_call" | custom-call | flops 12884901888 | bytes 17301504 | tf_op jit(solution)/shard_map/context_and_value_part/pallas_call | solution.py:563
  136.6 0.0 copy-done.1
  136.6 8.1 %convolution_convert_fusion = bf16[1024,1024]{0,1:T(8,128)(2,1)} fusion(bf16[2048,1024]{1,0:T(8,128)(2,1)} %get-tuple-element.22, bf16[2048,1024]{1,0:T(8,128)(2,1)S(1)} %copy-done.1), kind=kOutput, calls=%fused_computation | convolution fusion | flops 4296015872 | bytes 10485760 | tf_op jit(solution)/shard_map/dot_general | solution.py:27
  144.7 53.1 %query_and_key_part.1 = (bf16[1024,1024]{1,0:T(8,128)(2,1)}, bf16[2048,1024]{1,0:T(8,128)(2,1)}, bf16[64,1024]{1,0:T(8,128)(2,1)}, f32[64,1024]{1,0:T(8,128)}) custom-call(bf16[1024,1024]{1,0:T(8,128)(2,1)} %bitcast.27, bf16[1024,1024]{1,0:T(8,128)(2,1)} %convolution_convert_fusion.1.d_ref, bf16[2112,1024]{1,0:T(8,128)(2,1)} %get-tuple-element.19.k_ref, ...), custom_call_target="tpu_custom_call" | custom-call | flops 17179869184 | bytes 17301504 | tf_op jit(solution)/shard_map/query_and_key_part/pallas_call | solution.py:566
  197.8 1.1 copy.18
  198.8 0.9 reshape.59
  199.7 3.7 %all-to-all-start = ((bf16[16,2,2048]{2,1,0:T(2,128)(2,1)}), bf16[16,2,2048]{2,1,0:T(2,128)(2,1)S(1)}, u32[]{:S(2)}, u32[]{:S(2)}) async-start(bf16[16,2,2048]{2,1,0:T(2,128)(2,1)} %reshape.59), calls=%async_computation | async-start | bytes 262144 | tf_op jit(solution)/shard_map/all_to_all | solution.py:574
  203.4 0.0 copy-start.4
  203.4 0.0 copy-start.7
  203.5 49.9 %reduce_query_and_key.1 = (bf16[64,1024]{1,0:T(8,128)(2,1)}, f32[64,1024]{1,0:T(8,128)}) custom-call(bf16[2,2,2,2,64,1024]{5,4,3,2,1,0:T(8,128)(2,1)} %bitcast.28, bf16[2048,1024]{1,0:T(8,128)(2,1)} %reshape.44.x_ref, bf16[2048,1024]{1,0:T(8,128)(2,1)} %get-tuple-element.25.g_ref), custom_call_target="tpu_custom_call" | custom-call | flops 4429185024 | bytes 17301504 | tf_op jit(solution)/shard_map/reduce_query_and_key/pallas_call | solution.py:572
  253.4 0.0 copy-done.4
  253.4 0.0 copy-done.7
  253.4 1.2 fusion
  254.6 0.0 copy-start.6
  254.6 0.0 all-to-all-done
  254.6 0.2 reshape.60
  254.8 0.0 copy-start.3
  254.9 0.0 copy-start.2
  254.9 0.2 copy.17
  255.1 0.2 all_to_all.17
  255.3 1.1 fusion.3
  256.4 0.0 copy-done.6
  256.4 0.7 copy.23
  257.1 0.0 copy-done.3
  257.1 0.7 copy.24
  257.8 0.0 copy-done.2
  257.8 0.7 copy.25
  (3 shorter events, 0.1 us)
Async XLA Ops:
  0.6 71.6 %copy-start = (bf16[1024,1024]{1,0:T(8,128)(2,1)S(1)}, bf16[1024,1024]{1,0:T(8,128)(2,1)}, u32[]{:S(2)}) copy-start(bf16[1024,1024]{1,0:T(8,128)(2,1)} %param.12) | copy-start | bytes 6291460
  2.1 7.3 %copy-start.5 = (bf16[64,1024]{1,0:T(8,128)(2,1)S(1)}, bf16[64,1024]{1,0:T(8,128)(2,1)}, u32[]{:S(2)}) copy-start(bf16[64,1024]{1,0:T(8,128)(2,1)} %param.15) | copy-start | bytes 393220
  109.4 27.2 %copy-start.1 = (bf16[2048,1024]{1,0:T(8,128)(2,1)S(1)}, bf16[2048,1024]{1,0:T(8,128)(2,1)}, u32[]{:S(2)}) copy-start(bf16[2048,1024]{1,0:T(8,128)(2,1)} %reshape.44.x_ref) | copy-start | bytes 12582916
  199.7 54.9 %all-to-all-start = ((bf16[16,2,2048]{2,1,0:T(2,128)(2,1)}), bf16[16,2,2048]{2,1,0:T(2,128)(2,1)S(1)}, u32[]{:S(2)}, u32[]{:S(2)}) async-start(bf16[16,2,2048]{2,1,0:T(2,128)(2,1)} %reshape.59), calls=%async_computation | async-start | bytes 262144 | tf_op jit(solution)/shard_map/all_to_all | solution.py:574
  203.4 50.0 %copy-start.4 = (bf16[64,1024]{1,0:T(8,128)(2,1)S(1)}, bf16[64,1024]{1,0:T(8,128)(2,1)}, u32[]{:S(2)}) copy-start(bf16[64,1024]{1,0:T(8,128)(2,1)} %get-tuple-element.23) | copy-start | bytes 393220
  203.4 50.0 %copy-start.7 = (bf16[2,2,2,2,64,1152]{5,4,3,2,1,0:T(8,128)(2,1)S(1)}, bf16[2,2,2,2,64,1152]{5,4,3,2,1,0:T(8,128)(2,1)}, u32[]{:S(2)}) copy-start(bf16[2,2,2,2,64,1152]{5,4,3,2,1,0:T(8,128)(2,1)} %get-tuple-element.18) | copy-start | bytes 7077892
  254.6 1.8 copy-start.6
  254.8 2.2 copy-start.3
  254.9 2.9 %copy-start.2 = (f32[64,1024]{1,0:T(8,128)S(1)}, f32[64,1024]{1,0:T(8,128)}, u32[]{:S(2)}) copy-start(f32[64,1024]{1,0:T(8,128)} %get-tuple-element.37) | copy-start | bytes 786436

commit v4 on v3

--- a/solution.py
+++ b/solution.py
@@ -108,11 +108,10 @@
 
 
 class Reduce:
-    def __init__(self, me, n_bits, src, first_col, slots, send, recv):
-        self.me, self.order = me, list(range(n_bits))
+    def __init__(self, me, n_bits, order, src, slots, send, recv):
+        self.me, self.order = me, order
         self.bits = list(range(n_bits))[::-1]
         self.src, self.slots = src, slots
-        self.cols = pl.ds(first_col, slots[0].shape[-1])
         self.send, self.recv = send, recv
 
     def left(self, step):
@@ -124,7 +123,7 @@
             1 - bit_of(self.me, k) if bit == k else slice(None) for bit in self.left(step)
         )
         if step == 0:
-            part = self.src.at[index + (slice(None), self.cols)]
+            part = self.src.at[index]
         else:
             part = self.slots[step - 1].at[index]
         other = partner_of(self.me, k)
@@ -140,38 +139,29 @@
             chosen[k] = bit_of(self.me, k)
             at = tuple(chosen[bit] for bit in bits)
             if step == 0:
-                own = self.src[at + (slice(None), self.cols)]
+                own = self.src[at]
             else:
                 own = self.slots[step - 1][at]
             total = own.astype(jnp.float32) + self.slots[step][index].astype(jnp.float32)
             self.slots[step][index] = total.astype(jnp.bfloat16)
 
 
-class Staged:
-    def __init__(self, sums, starts, n_bits):
-        self.sums, self.starts, self.n_bits = sums, starts, n_bits
-        self.ticks = max(starts) + n_bits
-
-    def begin(self, at):
-        for one, start in zip(self.sums, self.starts):
-            if start == at:
-                one.copy(0).start()
-
-    def tick(self, at):
-        for one, start in zip(self.sums, self.starts):
-            step = at - start
-            if 0 <= step < self.n_bits:
-                one.finish(step)
-                if step + 1 < self.n_bits:
-                    one.copy(step + 1).start()
-        self.begin(at + 1)
-
-    def write(self, refs):
-        half = len(self.sums) // 2
-        for i, ref in enumerate(refs):
-            for j in range(half):
-                one = self.sums[i * half + j]
-                ref[:, one.cols] = one.slots[-1][...].astype(ref.dtype)
+    def advance(self, step):
+        self.finish(step)
+        if step + 1 < len(self.order):
+            self.copy(step + 1).start()
+
+
+def two_sums(me, n_bits, sources, rest):
+    send, recv = rest[-2:]
+    orders = (list(range(n_bits)), [0] + list(range(2, n_bits)) + [1])
+    return [
+        Reduce(
+            me, n_bits, orders[i], sources[i], rest[i * n_bits : (i + 1) * n_bits],
+            send.at[i], recv.at[i],
+        )
+        for i in range(2)
+    ]
 
 
 def slot_shapes(n_bits, rows, width):
@@ -182,16 +172,28 @@
 
 
 def project_kernel(
-    n_bits, chunk, q_ref, g_ref, x_ref, kw_ref, vw_ref, qo_ref, go_ref, k_ref, v_ref, send, recv
+    n_bits, chunk, q_ref, g_ref, x_any, kw_any, vw_any, qo_ref, go_ref, k_any, v_any,
+    x_ref, kw_ref, vw_ref, k_ref, v_ref, send, recv, local,
 ):
     me = lax.axis_index("tm")
+    loads = [
+        pltpu.make_async_copy(src, dst, local.at[i])
+        for i, (src, dst) in enumerate(((x_any, x_ref), (kw_any, kw_ref), (vw_any, vw_ref)))
+    ]
+    stores = [
+        pltpu.make_async_copy(src, dst, local.at[3 + i])
+        for i, (src, dst) in enumerate(((k_ref, k_any), (v_ref, v_any)))
+    ]
+    for load in loads:
+        load.start()
     greet([partner_of(me, k) for k in range(n_bits)])
-    order = list(range(n_bits))[::-1]
+    orders = (list(range(1, n_bits))[::-1] + [0], [1] + list(range(2, n_bits))[::-1] + [0])
     gathers = []
     for i, (mine, out) in enumerate(((q_ref, qo_ref), (g_ref, go_ref))):
         out[tuple(bit_of(me, k) for k in range(n_bits)[::-1])] = mine[...]
-        gathers.append(Gather(me, n_bits, order, out, send.at[i], recv.at[i]))
-    gathers[0].copy(0).start()
+        gathers.append(Gather(me, n_bits, orders[i], out, send.at[i], recv.at[i]))
+    for gather in gathers:
+        gather.copy(0).start()
     rows, width = x_ref.shape
     n_cols = width // GW
     pad = (k_ref.shape[0] - rows) // 2
@@ -213,20 +215,25 @@
         lax.fori_loop(0, rows // chunk, part, 0)
         return carry
 
-    lag = 2
-    ticks = n_bits + lag
-    for tick in range(ticks):
-        lax.fori_loop(n_cols * tick // ticks, n_cols * (tick + 1) // ticks, piece, 0)
-        for gather, start in zip(gathers, (0, lag)):
-            step = tick - start
-            if 0 <= step < n_bits:
-                gather.copy(step).wait()
-            if 0 <= step + 1 < n_bits:
+    for load in loads:
+        load.wait()
+    before = n_bits - 1
+    for step in range(n_bits):
+        if step < before:
+            lax.fori_loop(n_cols * step // before, n_cols * (step + 1) // before, piece, 0)
+        if step == before:
+            for store in stores:
+                store.start()
+        for gather in gathers:
+            gather.copy(step).wait()
+            if step + 1 < n_bits:
                 gather.copy(step + 1).start()
-
-
-def place(b, per, groups, g):
-    return b // per, pl.ds(lax.rem(b, per) * groups + g, 1)
+    for store in stores:
+        store.wait()
+
+
+def place(b, per, item):
+    return b // per, pl.ds(item * per + lax.rem(b, per), 1)
 
 
 def stats_kernel(
@@ -245,6 +252,8 @@
     def _():
         greet([lax.rem(me + i, n_dev) for i in range(1, n_dev)])
 
+    mine[g] = jnp.zeros(mine.shape[1:], jnp.float32)
+
     def step(b, carry):
         rows = pl.ds(pl.multiple_of(b * QB, QB), QB)
         keys = pl.ds(pl.multiple_of(b * QB * n_tok, QB * n_tok), n_keys)
@@ -255,46 +264,61 @@
         top = jnp.max(scores, axis=0, keepdims=True)
         expo = jnp.exp(scores - top)
         d_probs = dot(v_ref[keys, :], d4, NT)
-        owner, row = place(b, per, groups, g)
-        mine[owner, 0, row, :] = top
-        mine[owner, 1, row, :] = jnp.sum(expo, axis=0, keepdims=True)
-        mine[owner, 2, row, :] = jnp.sum(expo * d_probs, axis=0, keepdims=True)
+        sums = (top, jnp.sum(expo, axis=0, keepdims=True))
+        sums += (jnp.sum(expo * d_probs, axis=0, keepdims=True),)
+        for item, row in enumerate(sums):
+            owner, at = place(b, per, item)
+            mine[g, owner, at, :] = row
         return carry
 
     lax.fori_loop(0, total // QB, step, 0, unroll=UNROLL)
 
-    def there(i):
+    def there(h, i):
         other = lax.rem(me + i, n_dev)
-        return remote(mine.at[other], got.at[i], send.at[i], recv.at[i], other)
-
-    def back(i):
+        return remote(mine.at[h, other], got.at[h, i], send.at[h, i], recv.at[h, i], other)
+
+    def back(h, i):
         other = lax.rem(me + i, n_dev)
-        return remote(out_ref.at[me], out_ref.at[me], send_back.at[i], recv_back.at[i], other)
-
-    @pl.when(g == groups - 1)
-    def _():
+        own = out_ref.at[h, me]
+        return remote(own, own, send_back.at[h, i], recv_back.at[h, i], other)
+
+    def combine(h):
+        got[h, 0] = mine[h, me]
         for i in range(1, n_dev):
-            there(i).start()
-        got[0] = mine[me]
+            there(h, i).wait()
+        top = got[h, 0, :per]
         for i in range(1, n_dev):
-            there(i).wait()
-        top = got[0, 0]
-        for i in range(1, n_dev):
-            top = jnp.maximum(top, got[i, 0])
+            top = jnp.maximum(top, got[h, i, :per])
         norm = jnp.zeros_like(top)
         slope = jnp.zeros_like(top)
         for i in range(n_dev):
-            factor = jnp.exp(got[i, 0] - top)
-            norm = norm + factor * got[i, 1]
-            slope = slope + factor * got[i, 2]
+            factor = jnp.exp(got[h, i, :per] - top)
+            norm = norm + factor * got[h, i, per : 2 * per]
+            slope = slope + factor * got[h, i, 2 * per : 3 * per]
         inverse = 1.0 / norm
-        out_ref[me, 0] = top
-        out_ref[me, 1] = inverse
-        out_ref[me, 2] = slope * inverse
+        out_ref[h, me, :per] = top
+        out_ref[h, me, per : 2 * per] = inverse
+        out_ref[h, me, 2 * per : 3 * per] = slope * inverse
         for i in range(1, n_dev):
-            back(i).start()
-        for i in range(1, n_dev):
-            back(i).wait()
+            back(h, i).start()
+
+    for i in range(1, n_dev):
+        there(g, i).start()
+
+    @pl.when(g > 0)
+    def _():
+        combine(g - 1)
+
+    @pl.when(g == groups - 1)
+    def _():
+        combine(g)
+
+        def settle(h, carry):
+            for i in range(1, n_dev):
+                back(h, i).wait()
+            return carry
+
+        lax.fori_loop(0, groups, settle, 0)
         res_ref[...] = out_ref[...]
 
 
@@ -318,8 +342,9 @@
         d4 = spread(d_ref[rows, :], mask_b)
         allow = allowed(b, frame, ahead, off_ref[pl.ds(b, 1), :], total)
         scores = jnp.where(allow, dot(k_ref[keys, :], q4, NT) * SCALE, NEG)
-        owner, row = place(b, per, groups, g)
-        probs = jnp.exp(scores - st_ref[owner, 0, row, :]) * st_ref[owner, 1, row, :]
+        owner, top = place(b, per, 0)
+        inverse = place(b, per, 1)[1]
+        probs = jnp.exp(scores - st_ref[g, owner, top, :]) * st_ref[g, owner, inverse, :]
         probs_b = probs.astype(jnp.bfloat16)
         ctx[rows, :] = fold(dot(probs_b, v_ref[keys, :], TN))
         part = dot(probs_b, d4, NN)
@@ -346,12 +371,13 @@
     groups = pl.num_programs(0)
     per = total // QB // n_dev
     me = lax.axis_index("tm")
-    staged = Staged(four_sums(me, n_bits, (a_ref, b_ref), rest), (0, 1, 2, 3), n_bits)
+    sums = two_sums(me, n_bits, (a_ref, b_ref), rest)
 
     @pl.when(g == 0)
     def _():
         greet([partner_of(me, k) for k in range(n_bits)])
-        staged.begin(0)
+        for one in sums:
+            one.copy(0).start()
 
     def step(b, carry):
         rows = pl.ds(pl.multiple_of(b * QB, QB), QB)
@@ -362,69 +388,62 @@
         allow = allowed(b, frame, ahead, off_ref[pl.ds(b, 1), :], total)
         k_blk = k_ref[keys, :]
         scores = jnp.where(allow, dot(k_blk, q4, NT) * SCALE, NEG)
-        owner, row = place(b, per, groups, g)
-        probs = jnp.exp(scores - st_ref[owner, 0, row, :]) * st_ref[owner, 1, row, :]
+        owner, top = place(b, per, 0)
+        inverse = place(b, per, 1)[1]
+        probs = jnp.exp(scores - st_ref[g, owner, top, :]) * st_ref[g, owner, inverse, :]
         d_probs = dot(v_ref[keys, :], d4, NT)
-        d_scores = probs * (d_probs - st_ref[owner, 2, row, :]) * SCALE
+        d_scores = probs * (d_probs - st_ref[g, owner, place(b, per, 2)[1], :]) * SCALE
         d_scores = d_scores.astype(jnp.bfloat16)
         dq_ref[rows, :] = fold(dot(d_scores, k_blk, TN)).astype(jnp.bfloat16)
         part = dot(d_scores, q4, NN)
         acc[pl.ds(first, ahead_rows), :] = (carry + part[:ahead_rows]).astype(jnp.bfloat16)
         return part[ahead_rows:]
 
-    n_groups = b_ref.shape[-1] // GW
-    points = 2 * n_groups
-    half = total // QB // 2
-    tail = jnp.zeros((ahead_rows, GW), jnp.float32)
-    for side in range(2):
-        tail = lax.fori_loop(side * half, (side + 1) * half, step, tail, unroll=UNROLL)
-        for at in range(side, points, 2):
-
-            @pl.when(g == at // 2)
-            def _(at=at):
-                last = at + 1 if at + 1 < points else staged.ticks
-                for now in range(at, min(last, staged.ticks)):
-                    staged.tick(now)
-
+    zero = jnp.zeros((ahead_rows, GW), jnp.float32)
+    tail = lax.fori_loop(0, total // QB, step, zero, unroll=UNROLL)
     acc[total * n_tok :, :] = tail.astype(jnp.bfloat16)
     g_ref[...] = acc[pad : pad + total * n_tok, :]
 
+    n_groups = b_ref.shape[-1] // GW
+    for at in range(n_groups):
+
+        @pl.when(g == at)
+        def _(at=at):
+            last = at + 1 if at + 1 < n_groups else n_bits
+            for now in range(at, min(last, n_bits)):
+                for one in sums:
+                    one.advance(now)
+
     @pl.when(g == n_groups - 1)
     def _():
-        staged.write((ao_ref, bo_ref))
-
-
-def four_sums(me, n_bits, sources, rest):
-    send, recv = rest[-2:]
-    sums = []
-    for i in range(4):
-        slots = rest[i * n_bits : (i + 1) * n_bits]
-        first_col = (i % 2) * slots[0].shape[-1]
-        source = sources[i // 2]
-        sums.append(Reduce(me, n_bits, source, first_col, slots, send.at[i], recv.at[i]))
-    return sums
+        ao_ref[...] = sums[0].slots[-1][...]
+        bo_ref[...] = sums[1].slots[-1][...].astype(jnp.float32)
 
 
 def reduce_kernel(n_bits, a_ref, x_ref, g_ref, ao_ref, bo_ref, term, *rest):
     me = lax.axis_index("tm")
-    staged = Staged(four_sums(me, n_bits, (a_ref, term), rest), (0, 1, 2, 4), n_bits)
+    first, second = two_sums(me, n_bits, (a_ref, term), rest)
     greet([partner_of(me, k) for k in range(n_bits)])
-    staged.begin(0)
+    first.copy(0).start()
     width = x_ref.shape[1]
     own = term.shape[-2]
-    half = width // 2
-    for tick in range(staged.ticks):
-        if tick < 4:
-            cols = slice(tick // 2 * half, (tick // 2 + 1) * half)
-            for first in range(tick % 2 * half, (tick % 2 + 1) * half, GW):
-                product = dot(x_ref[:, first : first + GW], g_ref[:, cols], TN)
-                product = product.astype(jnp.bfloat16)
-                for i in range(GW // own):
-                    owner = first // own + i
-                    index = tuple((owner >> k) % 2 for k in range(n_bits)[::-1])
-                    term[index + (slice(None), cols)] = product[i * own : (i + 1) * own]
-        staged.tick(tick)
-    staged.write((ao_ref, bo_ref))
+    for col in range(0, width, GW):
+        product = dot(x_ref[:, col : col + GW], g_ref[...], TN).astype(jnp.bfloat16)
+        for i in range(GW // own):
+            owner = col // own + i
+            index = tuple((owner >> k) % 2 for k in range(n_bits)[::-1])
+            term[index] = product[i * own : (i + 1) * own]
+        if col == GW:
+            first.advance(0)
+    second.copy(0).start()
+    second.advance(0)
+    first.advance(1)
+    for step in range(2, n_bits):
+        first.advance(step)
+        second.advance(step - 1)
+    second.advance(n_bits - 1)
+    ao_ref[...] = first.slots[-1][...]
+    bo_ref[...] = second.slots[-1][...].astype(jnp.float32)
 
 
 def row_chunk(rows):
@@ -446,8 +465,9 @@
     part_like = jax.ShapeDtypeStruct((total * n_tok, width), jnp.bfloat16)
     by_part = pl.BlockSpec((total * n_tok, GW), lambda g: (0, g))
     key_acc = pltpu.VMEM((key_rows, GW), jnp.bfloat16)
-    stat = (n_dev, 3, blocks // n_dev * groups, LANES)
-    sems = [pltpu.SemaphoreType.DMA((4, n_bits))] * 2
+    stat = (groups, n_dev, -(-3 * (blocks // n_dev) // 8) * 8, LANES)
+    sems = [pltpu.SemaphoreType.DMA((2, n_bits))] * 2
+    anywhere = pl.BlockSpec(memory_space=pl.ANY)
     limit = 56 * 1024 * 1024
     unit = 2 * groups * blocks * (QB + 2 * W) * n_tok * LANES * GW
     common = [by_query, by_query, by_key, by_key, by_offset]
@@ -468,12 +488,16 @@
 
     project = pl.pallas_call(
         functools.partial(project_kernel, n_bits, row_chunk(total * n_tok)),
-        in_specs=[whole] * 5,
-        out_specs=[whole] * 4,
+        in_specs=[whole] * 2 + [anywhere] * 3,
+        out_specs=[whole] * 2 + [anywhere] * 2,
         out_shape=[
             shape(bits + (here, width)), shape(bits + (here, width + 128)), key_like, key_like
         ],
-        scratch_shapes=sems,
+        scratch_shapes=[pltpu.VMEM((total * n_tok, width), jnp.bfloat16)]
+        + [pltpu.VMEM((width, width), jnp.bfloat16)] * 2
+        + [pltpu.VMEM((key_rows, width), jnp.bfloat16)] * 2
+        + sems
+        + [pltpu.SemaphoreType.DMA((5,))],
         compiler_params=params(0),
         cost_estimate=cost(4 * key_rows * width * width),
         name="gather_and_project",
@@ -485,7 +509,7 @@
         out_specs=whole,
         out_shape=shape(stat, jnp.float32),
         scratch_shapes=[pltpu.VMEM(stat, jnp.float32)] * 3
-        + [pltpu.SemaphoreType.DMA((n_dev,))] * 4,
+        + [pltpu.SemaphoreType.DMA((groups, n_dev))] * 4,
         compiler_params=params(1),
         cost_estimate=cost(8 * unit),
         name="softmax_stats",
@@ -511,8 +535,8 @@
             shape((total, width)), part_like, shape((own, total)), shape((own, width), jnp.float32)
         ],
         scratch_shapes=[key_acc]
-        + slot_shapes(n_bits, own, total // 2) * 2
-        + slot_shapes(n_bits, own, width // 2) * 2
+        + slot_shapes(n_bits, own, total)
+        + slot_shapes(n_bits, own, width)
         + sems,
         compiler_params=params(2),
         cost_estimate=cost(16 * unit),
@@ -524,8 +548,8 @@
         out_specs=[whole] * 2,
         out_shape=[shape((here, width)), shape((own, width), jnp.float32)],
         scratch_shapes=[pltpu.VMEM(bits + (own, width), jnp.bfloat16)]
-        + slot_shapes(n_bits, here, width // 2) * 2
-        + slot_shapes(n_bits, own, width // 2) * 2
+        + slot_shapes(n_bits, here, width)
+        + slot_shapes(n_bits, own, width)
         + sems,
         compiler_params=params(3),
         cost_estimate=cost(2 * key_rows * width * width),

time: 259 us -> 249 us (0.961)
  Pallas kernels: 222 us -> 212 us
    pallas_call x1, Pallas kernels: 60.1 us -> 46.7 us  [shards(): project(queries, grad_wide, flat, key_weight, value_weight)]
    pallas_call x1, Pallas kernels: 49.9 us -> 57.8 us  [shards(): reduce(d_query.reshape(bits + (rows_here, width)), flat, key_part)]
  transfers between devices with their start and end apart: 1 -> 1, of which waited for: 0 -> 0; matrix products, arithmetic and copies ran while one was open for 0% -> 0% of each run, Pallas kernels for 19% -> 23%
where the time goes in v4:
time: 249 us
  Pallas kernels  212 us (85%)
  matrix products  15.7 us (6%)
  local copies, waits for them, and re-layouts  13.9 us (6%)
  starting transfers between devices  3.94 us (2%)
    pallas_call x1, Pallas kernels, shards(): reduce(d_query.reshape(bits + (rows_here, width)), flat, key_part)  57.8 us
    pallas_call x1, Pallas kernels, shards(): key(*common, combined, context_t.reshape(bits + (own, total)), value_term...  50.5 us
    pallas_call x1, Pallas kernels, shards(): project(queries, grad_wide, flat, key_weight, value_weight)  46.7 us
    pallas_call x1, Pallas kernels, shards(): combined = stats(*common)  30.1 us
    pallas_call x1, Pallas kernels, shards(): context_t, value_part = value(*common, combined)  27.3 us
    dot_general x4, matrix products, dot(): return lax.dot_general(a, b, dims, preferred_element_type=jnp.float32)  15.7 us
    reshape x1, local copies, waits for them, and re-layouts, shards(): flat = exo_tokens.reshape(-1, width)  7.26 us
  transfers between devices with their start and end apart: 1, of which 0 were waited for; matrix products, arithmetic and copies ran while one was open for 0% of the time, Pallas kernels for 23%

profile of v4, /device:TPU:0, one launch (start us, length us, event | category | flops | bytes accessed | tf_op | source)
XLA Modules:
  0.0 248.9 jit_solution(13608621829077141078)
XLA Ops:
  0.6 0.0 copy-start
  0.6 0.8 convert_element_type.35
  1.5 0.7 convert_element_type.37
  2.1 0.0 copy-start.5
  2.1 7.3 %reshape.44.x_any.x_ref = bf16[2048,1024]{1,0:T(8,128)(2,1)} reshape(bf16[1024,2,1024]{2,1,0:T(2,128)(2,1)} %param.8) | data formatting | bytes 8388608 | tf_op jit(solution)/shard_map/reshape | solution.py:573
  9.4 0.0 copy-done.5
  9.4 0.1 multiply_convert_fusion
  9.5 0.1 broadcast_in_dim.4
  9.5 0.7 pad_maximum_fusion.g_ref
  10.2 46.7 %gather_and_project.1 = (bf16[2,2,2,2,64,1024]{5,4,3,2,1,0:T(8,128)(2,1)}, bf16[2,2,2,2,64,1152]{5,4,3,2,1,0:T(8,128)(2,1)}, bf16[2112,1024]{1,0:T(8,128)(2,1)}, bf16[2112,1024]{1,0:T(8,128)(2,1)}) custom-call(bf16[64,1024]{1,0:T(8,128)(2,1)} %q_ref.1, bf16[64,1152]{1,0:T(8,128)(2,1)} %pad_maximum_fusion.g_ref, bf16[2048,1024]{1,0:T(8,128)(2,1)} %reshape.44.x_any.x_ref, ...), custom_call_target="tpu_custom_call" | custom-call | flops 8858370048 | bytes 17301504 | tf_op jit(solution)/shard_map/gather_and_project/pallas_call | solution.py:577
  56.9 1.0 slice.9
  57.9 0.1 copy.19
  58.1 0.1 reshape.51
  58.2 0.7 reshape.47.off_ref
  58.9 0.0 copy-done
  58.9 5.4 %convolution_convert_fusion.1.d_ref = bf16[1024,1024]{1,0:T(8,128)(2,1)} fusion(bf16[1024,1024]{1,0:T(8,128)(2,1)S(1)} %copy-done, bf16[1024,1152]{1,0:T(8,128)(2,1)} %bitcast.23), kind=kOutput, calls=%fused_computation.1 | convolution fusion | flops 2148532224 | bytes 6291456 | tf_op jit(solution)/shard_map/dot_general | solution.py:27
  64.2 30.1 %softmax_stats.1.st_ref = f32[4,16,8,128]{3,2,1,0:T(8,128)} custom-call(bf16[1024,1024]{1,0:T(8,128)(2,1)} %bitcast.25, bf16[1024,1024]{1,0:T(8,128)(2,1)} %convolution_convert_fusion.1.d_ref, bf16[2112,1024]{1,0:T(8,128)(2,1)} %get-tuple-element.19.k_ref, bf16[2112,1024]{1,0:T(8,128)(2,1)} %get-tuple-element.20.v_ref, s32[32,128]{1,0:T(8,128)} %reshape.47.off_ref), custom_call_target="tpu_custom_call" | custom-call | flops 8589934592 | bytes 17301504 | tf_op jit(solution)/shard_map/softmax_stats/pallas_call | solution.py:586
  94.3 0.0 copy-start.1
  94.3 27.3 %context_and_value_part.1 = (bf16[1024,1024]{1,0:T(8,128)(2,1)}, bf16[2048,1024]{1,0:T(8,128)(2,1)}) custom-call(bf16[1024,1024]{1,0:T(8,128)(2,1)} %bitcast.26, bf16[1024,1024]{1,0:T(8,128)(2,1)} %convolution_convert_fusion.1.d_ref, bf16[2112,1024]{1,0:T(8,128)(2,1)} %get-tuple-element.19.k_ref, bf16[2112,1024]{1,0:T(8,128)(2,1)} %get-tuple-element.20.v_ref, ...), custom_call_target="tpu_custom_call" | custom-call | flops 12884901888 | bytes 17301504 | tf_op jit(solution)/shard_map/context_and_value_part/pallas_call | solution.py:587
  121.6 0.0 copy-done.1
  121.6 8.1 %convolution_convert_fusion = bf16[1024,1024]{0,1:T(8,128)(2,1)} fusion(bf16[2048,1024]{1,0:T(8,128)(2,1)} %get-tuple-element.22, bf16[2048,1024]{1,0:T(8,128)(2,1)S(1)} %copy-done.1), kind=kOutput, calls=%fused_computation | convolution fusion | flops 4296015872 | bytes 10485760 | tf_op jit(solution)/shard_map/dot_general | solution.py:27
  129.7 50.5 %query_and_key_part.1 = (bf16[1024,1024]{1,0:T(8,128)(2,1)}, bf16[2048,1024]{1,0:T(8,128)(2,1)}, bf16[64,1024]{1,0:T(8,128)(2,1)}, f32[64,1024]{1,0:T(8,128)}) custom-call(bf16[1024,1024]{1,0:T(8,128)(2,1)} %bitcast.27, bf16[1024,1024]{1,0:T(8,128)(2,1)} %convolution_convert_fusion.1.d_ref, bf16[2112,1024]{1,0:T(8,128)(2,1)} %get-tuple-element.19.k_ref, ...), custom_call_target="tpu_custom_call" | custom-call | flops 17179869184 | bytes 17301504 | tf_op jit(solution)/shard_map/query_and_key_part/pallas_call | solution.py:590
  180.1 1.1 copy.18
  181.2 0.9 reshape.59
  182.1 3.9 %all-to-all-start = ((bf16[16,2,2048]{2,1,0:T(2,128)(2,1)}), bf16[16,2,2048]{2,1,0:T(2,128)(2,1)S(1)}, u32[]{:S(2)}, u32[]{:S(2)}) async-start(bf16[16,2,2048]{2,1,0:T(2,128)(2,1)} %reshape.59), calls=%async_computation | async-start | bytes 262144 | tf_op jit(solution)/shard_map/all_to_all | solution.py:598
  186.1 0.0 copy-start.4
  186.1 0.0 copy-start.7
  186.1 57.8 %reduce_query_and_key.1 = (bf16[64,1024]{1,0:T(8,128)(2,1)}, f32[64,1024]{1,0:T(8,128)}) custom-call(bf16[2,2,2,2,64,1024]{5,4,3,2,1,0:T(8,128)(2,1)} %bitcast.28, bf16[2048,1024]{1,0:T(8,128)(2,1)} %reshape.44.x_any.x_ref, bf16[2048,1024]{1,0:T(8,128)(2,1)} %get-tuple-element.25.g_ref), custom_call_target="tpu_custom_call" | custom-call | flops 4429185024 | bytes 17301504 | tf_op jit(solution)/shard_map/reduce_query_and_key/pallas_call | solution.py:596
  243.9 0.0 copy-done.4
  243.9 0.0 copy-done.7
  243.9 1.2 fusion
  245.1 0.0 copy-start.6
  245.1 0.0 all-to-all-done
  245.1 0.2 reshape.60
  245.3 0.0 copy-start.3
  245.3 0.0 copy-start.2
  245.3 0.2 copy.17
  245.5 0.2 all_to_all.17
  245.7 1.1 fusion.3
  246.9 0.0 copy-done.6
  246.9 0.7 copy.23
  247.5 0.0 copy-done.3
  247.5 0.7 copy.24
  248.2 0.0 copy-done.2
  248.2 0.7 copy.25
  (3 shorter events, 0.1 us)
Async XLA Ops:
  0.6 58.2 %copy-start = (bf16[1024,1024]{1,0:T(8,128)(2,1)S(1)}, bf16[1024,1024]{1,0:T(8,128)(2,1)}, u32[]{:S(2)}) copy-start(bf16[1024,1024]{1,0:T(8,128)(2,1)} %param.12) | copy-start | bytes 6291460
  2.1 7.3 %copy-start.5 = (bf16[64,1024]{1,0:T(8,128)(2,1)S(1)}, bf16[64,1024]{1,0:T(8,128)(2,1)}, u32[]{:S(2)}) copy-start(bf16[64,1024]{1,0:T(8,128)(2,1)} %param.15) | copy-start | bytes 393220
  94.3 27.3 %copy-start.1 = (bf16[2048,1024]{1,0:T(8,128)(2,1)S(1)}, bf16[2048,1024]{1,0:T(8,128)(2,1)}, u32[]{:S(2)}) copy-start(bf16[2048,1024]{1,0:T(8,128)(2,1)} %reshape.44.x_any.x_ref) | copy-start | bytes 12582916
  182.1 63.0 %all-to-all-start = ((bf16[16,2,2048]{2,1,0:T(2,128)(2,1)}), bf16[16,2,2048]{2,1,0:T(2,128)(2,1)S(1)}, u32[]{:S(2)}, u32[]{:S(2)}) async-start(bf16[16,2,2048]{2,1,0:T(2,128)(2,1)} %reshape.59), calls=%async_computation | async-start | bytes 262144 | tf_op jit(solution)/shard_map/all_to_all | solution.py:598
  186.1 57.8 %copy-start.4 = (bf16[64,1024]{1,0:T(8,128)(2,1)S(1)}, bf16[64,1024]{1,0:T(8,128)(2,1)}, u32[]{:S(2)}) copy-start(bf16[64,1024]{1,0:T(8,128)(2,1)} %get-tuple-element.23) | copy-start | bytes 393220
  186.1 57.8 %copy-start.7 = (bf16[2,2,2,2,64,1152]{5,4,3,2,1,0:T(8,128)(2,1)S(1)}, bf16[2,2,2,2,64,1152]{5,4,3,2,1,0:T(8,128)(2,1)}, u32[]{:S(2)}) copy-start(bf16[2,2,2,2,64,1152]{5,4,3,2,1,0:T(8,128)(2,1)} %get-tuple-element.18) | copy-start | bytes 7077892
  245.1 1.8 copy-start.6
  245.3 2.2 copy-start.3
  245.3 2.9 %copy-start.2 = (f32[64,1024]{1,0:T(8,128)S(1)}, f32[64,1024]{1,0:T(8,128)}, u32[]{:S(2)}) copy-start(f32[64,1024]{1,0:T(8,128)} %get-tuple-element.37) | copy-start | bytes 786436

commit v5 on v4

--- a/solution.py
+++ b/solution.py
@@ -108,8 +108,9 @@
 
 
 class Reduce:
-    def __init__(self, me, n_bits, order, src, slots, send, recv):
+    def __init__(self, me, n_bits, order, src, first_col, slots, send, recv):
         self.me, self.order = me, order
+        self.cols = pl.ds(first_col, slots[0].shape[-1])
         self.bits = list(range(n_bits))[::-1]
         self.src, self.slots = src, slots
         self.send, self.recv = send, recv
@@ -123,7 +124,7 @@
             1 - bit_of(self.me, k) if bit == k else slice(None) for bit in self.left(step)
         )
         if step == 0:
-            part = self.src.at[index]
+            part = self.src.at[index + (slice(None), self.cols)]
         else:
             part = self.slots[step - 1].at[index]
         other = partner_of(self.me, k)
@@ -139,7 +140,7 @@
             chosen[k] = bit_of(self.me, k)
             at = tuple(chosen[bit] for bit in bits)
             if step == 0:
-                own = self.src[at]
+                own = self.src[at + (slice(None), self.cols)]
             else:
                 own = self.slots[step - 1][at]
             total = own.astype(jnp.float32) + self.slots[step][index].astype(jnp.float32)
@@ -157,7 +158,7 @@
     orders = (list(range(n_bits)), [0] + list(range(2, n_bits)) + [1])
     return [
         Reduce(
-            me, n_bits, orders[i], sources[i], rest[i * n_bits : (i + 1) * n_bits],
+            me, n_bits, orders[i], sources[i], 0, rest[i * n_bits : (i + 1) * n_bits],
             send.at[i], recv.at[i],
         )
         for i in range(2)
@@ -420,30 +421,62 @@
         bo_ref[...] = sums[1].slots[-1][...].astype(jnp.float32)
 
 
+class Staged:
+    def __init__(self, sums, starts, n_bits):
+        self.sums, self.starts, self.n_bits = sums, starts, n_bits
+        self.ticks = max(starts) + n_bits
+
+    def begin(self, at):
+        for one, start in zip(self.sums, self.starts):
+            if start == at:
+                one.copy(0).start()
+
+    def tick(self, at):
+        for one, start in zip(self.sums, self.starts):
+            if 0 <= at - start < self.n_bits:
+                one.advance(at - start)
+        self.begin(at + 1)
+
+    def write(self, refs):
+        half = len(self.sums) // 2
+        for i, ref in enumerate(refs):
+            for one in self.sums[i * half : (i + 1) * half]:
+                ref[:, one.cols] = one.slots[-1][...].astype(ref.dtype)
+
+
+def four_sums(me, n_bits, sources, rest):
+    send, recv = rest[-2:]
+    order = list(range(n_bits))
+    sums = []
+    for i in range(4):
+        slots = rest[i * n_bits : (i + 1) * n_bits]
+        first_col = (i % 2) * slots[0].shape[-1]
+        source = sources[i // 2]
+        sums.append(Reduce(me, n_bits, order, source, first_col, slots, send.at[i], recv.at[i]))
+    return sums
+
+
 def reduce_kernel(n_bits, a_ref, x_ref, g_ref, ao_ref, bo_ref, term, *rest):
     me = lax.axis_index("tm")
-    first, second = two_sums(me, n_bits, (a_ref, term), rest)
+    staged = Staged(four_sums(me, n_bits, (a_ref, term), rest), (0, 1, 2, 3), n_bits)
     greet([partner_of(me, k) for k in range(n_bits)])
-    first.copy(0).start()
+    staged.begin(0)
     width = x_ref.shape[1]
     own = term.shape[-2]
-    for col in range(0, width, GW):
-        product = dot(x_ref[:, col : col + GW], g_ref[...], TN).astype(jnp.bfloat16)
-        for i in range(GW // own):
-            owner = col // own + i
-            index = tuple((owner >> k) % 2 for k in range(n_bits)[::-1])
-            term[index] = product[i * own : (i + 1) * own]
-        if col == GW:
-            first.advance(0)
-    second.copy(0).start()
-    second.advance(0)
-    first.advance(1)
-    for step in range(2, n_bits):
-        first.advance(step)
-        second.advance(step - 1)
-    second.advance(n_bits - 1)
-    ao_ref[...] = first.slots[-1][...]
-    bo_ref[...] = second.slots[-1][...].astype(jnp.float32)
+    half = width // 2
+    pieces = ((0, 1), (2,), (3,))
+    for tick in range(staged.ticks):
+        for piece in pieces[tick] if tick < len(pieces) else ():
+            cols = slice(piece // 2 * half, (piece // 2 + 1) * half)
+            for first in range(piece % 2 * half, (piece % 2 + 1) * half, GW):
+                product = dot(x_ref[:, first : first + GW], g_ref[:, cols], TN)
+                product = product.astype(jnp.bfloat16)
+                for i in range(GW // own):
+                    owner = first // own + i
+                    index = tuple((owner >> k) % 2 for k in range(n_bits)[::-1])
+                    term[index + (slice(None), cols)] = product[i * own : (i + 1) * own]
+        staged.tick(tick)
+    staged.write((ao_ref, bo_ref))
 
 
 def row_chunk(rows):
@@ -548,9 +581,9 @@
         out_specs=[whole] * 2,
         out_shape=[shape((here, width)), shape((own, width), jnp.float32)],
         scratch_shapes=[pltpu.VMEM(bits + (own, width), jnp.bfloat16)]
-        + slot_shapes(n_bits, here, width)
-        + slot_shapes(n_bits, own, width)
-        + sems,
+        + slot_shapes(n_bits, here, width // 2) * 2
+        + slot_shapes(n_bits, own, width // 2) * 2
+        + [pltpu.SemaphoreType.DMA((4, n_bits))] * 2,
         compiler_params=params(3),
         cost_estimate=cost(2 * key_rows * width * width),
         name="reduce_query_and_key",

time: 249 us -> 238 us (0.956)
  Pallas kernels: 212 us -> 201 us
    pallas_call x1, Pallas kernels: 57.8 us -> 46.7 us  [shards(): reduce(d_query.reshape(bits + (rows_here, width)), flat, key_part)]
  transfers between devices with their start and end apart: 1 -> 1, of which waited for: 0 -> 0; matrix products, arithmetic and copies ran while one was open for 0% -> 0% of each run, Pallas kernels for 23% -> 20%
where the time goes in v5:
time: 238 us
  Pallas kernels  201 us (84%)
  matrix products  15.7 us (7%)
  local copies, waits for them, and re-layouts  13.9 us (6%)
  starting transfers between devices  3.94 us (2%)
    pallas_call x1, Pallas kernels, shards(): key(*common, combined, context_t.reshape(bits + (own, total)), value_term...  50.5 us
    pallas_call x1, Pallas kernels, shards(): reduce(d_query.reshape(bits + (rows_here, width)), flat, key_part)  46.7 us
    pallas_call x1, Pallas kernels, shards(): project(queries, grad_wide, flat, key_weight, value_weight)  46.7 us
    pallas_call x1, Pallas kernels, shards(): combined = stats(*common)  30.1 us
    pallas_call x1, Pallas kernels, shards(): context_t, value_part = value(*common, combined)  27.3 us
    dot_general x4, matrix products, dot(): return lax.dot_general(a, b, dims, preferred_element_type=jnp.float32)  15.7 us
    reshape x1, local copies, waits for them, and re-layouts, shards(): flat = exo_tokens.reshape(-1, width)  7.26 us
  transfers between devices with their start and end apart: 1, of which 0 were waited for; matrix products, arithmetic and copies ran while one was open for 0% of the time, Pallas kernels for 20%

profile of v5, /device:TPU:0, one launch (start us, length us, event | category | flops | bytes accessed | tf_op | source)
XLA Modules:
  0.0 237.9 jit_solution(10606288035041221006)
XLA Ops:
  0.6 0.0 copy-start
  0.6 0.8 convert_element_type.35
  1.5 0.7 convert_element_type.37
  2.1 0.0 copy-start.5
  2.1 7.3 %reshape.44.x_any.x_ref = bf16[2048,1024]{1,0:T(8,128)(2,1)} reshape(bf16[1024,2,1024]{2,1,0:T(2,128)(2,1)} %param.8) | data formatting | bytes 8388608 | tf_op jit(solution)/shard_map/reshape | solution.py:606
  9.4 0.0 copy-done.5
  9.4 0.1 multiply_convert_fusion
  9.5 0.1 broadcast_in_dim.4
  9.5 0.7 pad_maximum_fusion.g_ref
  10.2 46.7 %gather_and_project.1 = (bf16[2,2,2,2,64,1024]{5,4,3,2,1,0:T(8,128)(2,1)}, bf16[2,2,2,2,64,1152]{5,4,3,2,1,0:T(8,128)(2,1)}, bf16[2112,1024]{1,0:T(8,128)(2,1)}, bf16[2112,1024]{1,0:T(8,128)(2,1)}) custom-call(bf16[64,1024]{1,0:T(8,128)(2,1)} %q_ref.1, bf16[64,1152]{1,0:T(8,128)(2,1)} %pad_maximum_fusion.g_ref, bf16[2048,1024]{1,0:T(8,128)(2,1)} %reshape.44.x_any.x_ref, ...), custom_call_target="tpu_custom_call" | custom-call | flops 8858370048 | bytes 17301504 | tf_op jit(solution)/shard_map/gather_and_project/pallas_call | solution.py:610
  56.9 1.0 slice.9
  57.9 0.1 copy.19
  58.1 0.1 reshape.51
  58.2 0.7 reshape.47.off_ref
  58.9 0.0 copy-done
  58.9 5.4 %convolution_convert_fusion.1.d_ref = bf16[1024,1024]{1,0:T(8,128)(2,1)} fusion(bf16[1024,1024]{1,0:T(8,128)(2,1)S(1)} %copy-done, bf16[1024,1152]{1,0:T(8,128)(2,1)} %bitcast.23), kind=kOutput, calls=%fused_computation.1 | convolution fusion | flops 2148532224 | bytes 6291456 | tf_op jit(solution)/shard_map/dot_general | solution.py:27
  64.2 30.1 %softmax_stats.1.st_ref = f32[4,16,8,128]{3,2,1,0:T(8,128)} custom-call(bf16[1024,1024]{1,0:T(8,128)(2,1)} %bitcast.25, bf16[1024,1024]{1,0:T(8,128)(2,1)} %convolution_convert_fusion.1.d_ref, bf16[2112,1024]{1,0:T(8,128)(2,1)} %get-tuple-element.19.k_ref, bf16[2112,1024]{1,0:T(8,128)(2,1)} %get-tuple-element.20.v_ref, s32[32,128]{1,0:T(8,128)} %reshape.47.off_ref), custom_call_target="tpu_custom_call" | custom-call | flops 8589934592 | bytes 17301504 | tf_op jit(solution)/shard_map/softmax_stats/pallas_call | solution.py:619
  94.3 0.0 copy-start.1
  94.3 27.3 %context_and_value_part.1 = (bf16[1024,1024]{1,0:T(8,128)(2,1)}, bf16[2048,1024]{1,0:T(8,128)(2,1)}) custom-call(bf16[1024,1024]{1,0:T(8,128)(2,1)} %bitcast.26, bf16[1024,1024]{1,0:T(8,128)(2,1)} %convolution_convert_fusion.1.d_ref, bf16[2112,1024]{1,0:T(8,128)(2,1)} %get-tuple-element.19.k_ref, bf16[2112,1024]{1,0:T(8,128)(2,1)} %get-tuple-element.20.v_ref, ...), custom_call_target="tpu_custom_call" | custom-call | flops 12884901888 | bytes 17301504 | tf_op jit(solution)/shard_map/context_and_value_part/pallas_call | solution.py:620
  121.6 0.0 copy-done.1
  121.6 8.1 %convolution_convert_fusion = bf16[1024,1024]{0,1:T(8,128)(2,1)} fusion(bf16[2048,1024]{1,0:T(8,128)(2,1)} %get-tuple-element.22, bf16[2048,1024]{1,0:T(8,128)(2,1)S(1)} %copy-done.1), kind=kOutput, calls=%fused_computation | convolution fusion | flops 4296015872 | bytes 10485760 | tf_op jit(solution)/shard_map/dot_general | solution.py:27
  129.7 50.5 %query_and_key_part.1 = (bf16[1024,1024]{1,0:T(8,128)(2,1)}, bf16[2048,1024]{1,0:T(8,128)(2,1)}, bf16[64,1024]{1,0:T(8,128)(2,1)}, f32[64,1024]{1,0:T(8,128)}) custom-call(bf16[1024,1024]{1,0:T(8,128)(2,1)} %bitcast.27, bf16[1024,1024]{1,0:T(8,128)(2,1)} %convolution_convert_fusion.1.d_ref, bf16[2112,1024]{1,0:T(8,128)(2,1)} %get-tuple-element.19.k_ref, ...), custom_call_target="tpu_custom_call" | custom-call | flops 17179869184 | bytes 17301504 | tf_op jit(solution)/shard_map/query_and_key_part/pallas_call | solution.py:623
  180.1 1.1 copy.18
  181.2 0.9 reshape.59
  182.1 3.9 %all-to-all-start = ((bf16[16,2,2048]{2,1,0:T(2,128)(2,1)}), bf16[16,2,2048]{2,1,0:T(2,128)(2,1)S(1)}, u32[]{:S(2)}, u32[]{:S(2)}) async-start(bf16[16,2,2048]{2,1,0:T(2,128)(2,1)} %reshape.59), calls=%async_computation | async-start | bytes 262144 | tf_op jit(solution)/shard_map/all_to_all | solution.py:631
  186.1 0.0 copy-start.4
  186.1 0.0 copy-start.7
  186.1 46.7 %reduce_query_and_key.1 = (bf16[64,1024]{1,0:T(8,128)(2,1)}, f32[64,1024]{1,0:T(8,128)}) custom-call(bf16[2,2,2,2,64,1024]{5,4,3,2,1,0:T(8,128)(2,1)} %bitcast.28, bf16[2048,1024]{1,0:T(8,128)(2,1)} %reshape.44.x_any.x_ref, bf16[2048,1024]{1,0:T(8,128)(2,1)} %get-tuple-element.25.g_ref), custom_call_target="tpu_custom_call" | custom-call | flops 4429185024 | bytes 17301504 | tf_op jit(solution)/shard_map/reduce_query_and_key/pallas_call | solution.py:629
  232.8 0.0 copy-done.4
  232.9 0.0 copy-done.7
  232.9 1.2 fusion
  234.0 0.0 copy-start.6
  234.0 0.0 all-to-all-done
  234.0 0.2 reshape.60
  234.3 0.0 copy-start.3
  234.3 0.0 copy-start.2
  234.3 0.2 copy.17
  234.5 0.2 all_to_all.17
  234.7 1.1 fusion.3
  235.8 0.0 copy-done.6
  235.8 0.7 copy.23
  236.5 0.0 copy-done.3
  236.5 0.7 copy.24
  237.2 0.0 copy-done.2
  237.2 0.7 copy.25
  (3 shorter events, 0.1 us)
Async XLA Ops:
  0.6 58.2 %copy-start = (bf16[1024,1024]{1,0:T(8,128)(2,1)S(1)}, bf16[1024,1024]{1,0:T(8,128)(2,1)}, u32[]{:S(2)}) copy-start(bf16[1024,1024]{1,0:T(8,128)(2,1)} %param.12) | copy-start | bytes 6291460
  2.1 7.3 %copy-start.5 = (bf16[64,1024]{1,0:T(8,128)(2,1)S(1)}, bf16[64,1024]{1,0:T(8,128)(2,1)}, u32[]{:S(2)}) copy-start(bf16[64,1024]{1,0:T(8,128)(2,1)} %param.15) | copy-start | bytes 393220
  94.3 27.3 %copy-start.1 = (bf16[2048,1024]{1,0:T(8,128)(2,1)S(1)}, bf16[2048,1024]{1,0:T(8,128)(2,1)}, u32[]{:S(2)}) copy-start(bf16[2048,1024]{1,0:T(8,128)(2,1)} %reshape.44.x_any.x_ref) | copy-start | bytes 12582916
  182.1 51.9 %all-to-all-start = ((bf16[16,2,2048]{2,1,0:T(2,128)(2,1)}), bf16[16,2,2048]{2,1,0:T(2,128)(2,1)S(1)}, u32[]{:S(2)}, u32[]{:S(2)}) async-start(bf16[16,2,2048]{2,1,0:T(2,128)(2,1)} %reshape.59), calls=%async_computation | async-start | bytes 262144 | tf_op jit(solution)/shard_map/all_to_all | solution.py:631
  186.1 46.8 %copy-start.4 = (bf16[64,1024]{1,0:T(8,128)(2,1)S(1)}, bf16[64,1024]{1,0:T(8,128)(2,1)}, u32[]{:S(2)}) copy-start(bf16[64,1024]{1,0:T(8,128)(2,1)} %get-tuple-element.23) | copy-start | bytes 393220
  186.1 46.8 %copy-start.7 = (bf16[2,2,2,2,64,1152]{5,4,3,2,1,0:T(8,128)(2,1)S(1)}, bf16[2,2,2,2,64,1152]{5,4,3,2,1,0:T(8,128)(2,1)}, u32[]{:S(2)}) copy-start(bf16[2,2,2,2,64,1152]{5,4,3,2,1,0:T(8,128)(2,1)} %get-tuple-element.18) | copy-start | bytes 7077892
  234.0 1.8 copy-start.6
  234.3 2.2 copy-start.3
  234.3 2.9 %copy-start.2 = (f32[64,1024]{1,0:T(8,128)S(1)}, f32[64,1024]{1,0:T(8,128)}, u32[]{:S(2)}) copy-start(f32[64,1024]{1,0:T(8,128)} %get-tuple-element.37) | copy-start | bytes 786436
